TPU v7x, 512 devices: a whole 4x8x8 slice. The times are simulated.
512 devices in a mesh: dom: 32 (over z, x), mode: 16 (over y, core).
Axes of the slice: x: 4, y: 8, z: 8, core: 2. Of those that a mesh axis runs over, the one named last changes fastest.
Arguments:
- shapes: bfloat16 [3, 8192, 4096], P(None, 'dom', 'mode'), may hold values from -6 to 6
- masses: float32 [8192], P('dom'), may hold values from 0.1 to 30, as said below
- spectral: float32 [3, 4096], replicated, may hold values from 2 to 16, as said below
- frequencies: float32 [4096], replicated, may hold values from 2 to 300, as said below
- damping: float32 [4096], replicated, may hold values from 0.015 to 0.03, as said below
- recovery: bfloat16 [2048, 8, 4, 3], P('dom'), may hold values from -1.75 to 1.75
- connectivity: int32 [2048, 4], P('dom'), may hold values from 0 to 383
- node_count: int32 [2048], P('dom'), may hold values from 2 to 4
- shared: int32 [2, 2048], P(None, 'dom'), may hold values from 0 to 255
Outputs:
- response: float32 [16384], P('dom')
Inputs may be any that keep to these rules, and one draw needn't show every extreme that they name: Positive node masses. Positive spectral displacements. Positive circular frequencies. Positive damping ratios. `connectivity`: codes below 256 are own nodes; the next 64 codes name the lower neighbour's upper list, the last 64 the upper neighbour's lower list. `shared`: local node numbers; entries may repeat.
All inputs are finite; a program needn't handle non-finite values.
Results may differ from a plain program's by a relative error of at most 0.0025.
Values may be sent and summed in bfloat16 or wider, within the bound.
A program may use at most 64 MiB of HBM per device.

v0:
```python
import jax
import jax.numpy as jnp
from jax import lax
from jax.sharding import PartitionSpec as P


def extended_2(block, sides, width):
    for axis, dim in sides:
        count = lax.axis_size(axis)
        forward = [(i, i + 1) for i in range(count - 1)]
        backward = [(target, source) for source, target in forward]
        low = lax.ppermute(
            lax.slice_in_dim(block, block.shape[dim] - width, None, axis=dim), axis, forward
        )
        high = lax.ppermute(lax.slice_in_dim(block, 0, width, axis=dim), axis, backward)
        block = jnp.concatenate([low, block, high], axis=dim)
    return block


def correlation_block(freq_rows, freq_cols, rate_rows, rate_cols):
    ratio = freq_cols[None, :] / freq_rows[:, None]
    ratio_sq = ratio * ratio
    rate_row = rate_rows[:, None]
    rate_col = rate_cols[None, :]
    top_part = (
        8.0
        * jnp.sqrt(rate_row * rate_col)
        * (rate_row + ratio * rate_col)
        * ratio
        * jnp.sqrt(ratio)
    )
    spread = 1.0 - ratio_sq
    bottom_part = (
        spread * spread
        + 4.0 * rate_row * rate_col * ratio * (1.0 + ratio_sq)
        + 4.0 * (rate_row * rate_row + rate_col * rate_col) * ratio_sq
    )
    return top_part / bottom_part


def block_terms(own_forces, own_start, far_forces, amplitudes, frequencies, damping):
    row_count = own_forces.shape[1]
    col_count = far_forces.shape[1]
    freq_rows = lax.dynamic_slice_in_dim(frequencies, own_start, row_count)
    rate_rows = lax.dynamic_slice_in_dim(damping, own_start, row_count)
    correlation = correlation_block(freq_rows, frequencies, rate_rows, damping)
    amp_rows = lax.dynamic_slice_in_dim(amplitudes, own_start, row_count, 1)
    weights = (amp_rows.T[:, :, None] * correlation[:, None, :] * amplitudes[None, :, :]).astype(
        jnp.bfloat16
    )
    weights = weights.reshape(row_count, 3 * col_count)
    projected = jnp.dot(own_forces, weights, preferred_element_type=jnp.float32)
    projected = projected.reshape(own_forces.shape[0], 3, col_count)
    far_wide = far_forces.astype(jnp.float32)
    return jnp.sum(projected * far_wide[:, None, :], axis=(1, 2))


def per_device(
    shapes, masses, spectral, frequencies, damping, recovery, connectivity, node_count, shared
):
    rim_width = shared.shape[1]
    block_width = shapes.shape[2]
    elem_count = connectivity.shape[0]
    slot_count = connectivity.shape[1]
    mode_index = lax.axis_index("mode")
    own_start = mode_index * block_width
    shape_wide = shapes.astype(jnp.float32)
    weighted = masses[None, :, None] * shape_wide
    lever_arm = jnp.sum(weighted, axis=1)
    general = jnp.sum(weighted * shape_wide, axis=(0, 1))
    lever_sum, general_sum = lax.psum((lever_arm, general), "dom")
    own_spectral = lax.dynamic_slice_in_dim(spectral, own_start, block_width, 1)
    local_amps = lever_sum / general_sum[None, :] * own_spectral
    amplitudes = lax.all_gather(local_amps, "mode", axis=1, tiled=True)
    outgoing = jnp.concatenate(
        [jnp.take(shapes, shared[0], axis=1), jnp.take(shapes, shared[1], axis=1)], axis=1
    )
    extended = extended_2(outgoing, (("dom", 1),), rim_width)
    node_table = jnp.concatenate(
        [shapes, extended[:, :rim_width], extended[:, 3 * rim_width :]], axis=1
    )
    gathered = jnp.take(node_table, connectivity.reshape(-1), axis=1).reshape(
        3, elem_count, slot_count, block_width
    )
    slot_live = (jnp.arange(slot_count)[None, :] < node_count[:, None]).astype(jnp.bfloat16)
    masked = recovery * slot_live[:, None, :, None]
    forces = jnp.einsum("ekna,aenm->ekm", masked, gathered, preferred_element_type=jnp.float32)
    forces = forces.astype(jnp.bfloat16).reshape(elem_count * recovery.shape[1], block_width)
    partial_value = block_terms(
        forces,
        own_start,
        lax.all_gather(forces, "mode", axis=1, tiled=True),
        amplitudes,
        frequencies,
        damping,
    )
    return lax.psum(partial_value, "mode")


def solution(mesh):
    in_specs = (
        P(None, "dom", "mode"),
        P("dom"),
        P(),
        P(),
        P(),
        P("dom", None, None, None),
        P("dom", None),
        P("dom"),
        P(None, "dom"),
    )
    out_specs = P("dom")
    return jax.shard_map(
        per_device, mesh=mesh, in_specs=in_specs, out_specs=out_specs, check_vma=False
    )
```

profile of v0, /device:TPU:1, one launch (start us, length us, event | category | flops | bytes accessed | tf_op | source)
XLA Modules:
  0.0 182.9 jit_solution(10090110753912843617)
XLA Ops:
  6.5 0.8 compare_and_fusion.1
  7.3 1.9 %gather_fusion.1 = bf16[64,3,256]{2,0,1:T(8,128)(2,1)S(1)} fusion(bf16[3,256,256]{2,1,0:T(8,128)(2,1)} %param.11, s32[1024]{0:T(1024)S(1)} %pad_clamp_fusion.2), kind=kCustom, calls=%fused_computation.clone | custom fusion | bytes 196864 | tf_op jit(solution)/shard_map/jit(_take)/gather | solution.py:76
  9.3 4.1 %collective-permute-start = (bf16[3,64,256]{2,1,0:T(8,128)(2,1)S(1)}, bf16[3,64,256]{2,1,0:T(8,128)(2,1)S(1)}, u32[]{:S(2)}, u32[]{:S(2)}) collective-permute-start(bf16[3,64,256]{2,1,0:T(8,128)(2,1)S(1)} %select_bitcast_fusion.1), channel_id=1, source_target_pairs={{0,16},{16,32},{32,48},{48,64},{64,80},{80,96},{96,112},{112,128},... | collective-permute-start | bytes 294920 | tf_op jit(solution)/shard_map/ppermute | solution.py:12
  13.4 1.9 %gather_fusion.2 = bf16[64,3,256]{2,0,1:T(8,128)(2,1)S(1)} fusion(bf16[3,256,256]{2,1,0:T(8,128)(2,1)} %param.11, s32[1024]{0:T(1024)S(1)} %pad_clamp_fusion.1), kind=kCustom, calls=%fused_computation.1.clone | custom fusion | bytes 196864 | tf_op jit(solution)/shard_map/jit(_take)/gather | solution.py:76
  15.4 1.3 collective-permute-start.1
  16.7 1.3 copy.14
  18.1 0.8 copy.17
  18.9 0.7 compare_and_fusion.2
  19.7 0.7 fusion.6
  20.3 0.8 broadcast_multiply_fusion.1
  21.1 0.2 copy.19
  21.6 0.6 pad_maximum_fusion
  22.1 1.2 gather_fusion
  23.3 1.3 fusion.1
  24.8 0.2 fusion.2
  25.0 68.9 %all-reduce = (f32[3,256]{1,0:T(4,128)S(1)}, f32[256]{0:T(256)S(1)}) all-reduce(f32[3,256]{1,0:T(4,128)S(1)} %get-tuple-element.7, f32[256]{0:T(256)S(1)} %get-tuple-element.6), channel_id=1, replica_groups=mesh['dom'=32,'mode'=16] {'dom'}, use_global_device_ids=true, to_apply=%region_1.3 | all-reduce | flops 1024 | bytes 8192 | tf_op jit(solution)/shard_map/psum | solution.py:71
  93.9 0.7 divide_multiply_fusion
  94.6 32.6 %all_gather.6 = f32[3,4096]{1,0:T(4,128)S(1)} all-gather(f32[3,256]{1,0:T(4,128)S(1)} %divide_multiply_fusion), channel_id=1, replica_groups=mesh['dom'=32,'mode'=16] {'mode'}, dimensions={1}, use_global_device_ids=true | all-gather | bytes 52224 | tf_op jit(solution)/shard_map/all_gather | solution.py:74
  127.3 5.0 %add_divide_fusion = f32[256,4096]{0,1:T(8,128)S(1)} fusion(f32[4096]{0:T(1024)S(1)} %mul.220, f32[256]{0:T(256)S(1)} %mul.219, f32[256]{0:T(256)S(1)} %get-tuple-element.10, f32[256]{0:T(256)S(1)} %dynamic_slice.15, f32[4096]{0:T(1024)S(1)} %copy-done.3, f32[4096]{0:T(1024)S(1)} %copy-done.2, f32[256]{0:T(256)S(1)} %get-tuple-element.11), kind=kLoop, calls=%fused_computation.7 | loop fusion | flops 22020096 | bytes 4247552 | tf_op jit(solution)/shard_map/div | solution.py:38
  132.4 1.0 broadcast_multiply_fusion
  133.4 4.6 %fusion = bf16[256,12288]{0,1:T(8,128)(2,1)} fusion(f32[256,3,4096]{0,2,1:T(8,128)S(1)} %broadcast_multiply_fusion, f32[12288]{0:T(1024)S(1)} %mul.227), kind=kLoop, calls=%fused_computation.5 | loop fusion | flops 6291456 | bytes 18923520 | tf_op jit(solution)/shard_map/convert_element_type | solution.py:48
  138.0 6.5 %convert_element_type.24 = f32[512,4096]{1,0:T(8,128)} convert(bf16[512,4096]{1,0:T(8,128)(2,1)} %all-gather.2.cloned.1.call-done) | non-fusion elementwise | flops 2097152 | bytes 12582912 | tf_op jit(solution)/shard_map/convert_element_type | solution.py:54
  144.5 7.9 %multiply_reduce_fusion = f32[512]{0:T(512)S(1)} fusion(f32[512,4096]{1,0:T(8,128)} %convert_element_type.24, bf16[3,4096,256]{2,1,0:T(8,128)(2,1)} %bitcast.35, bf16[64,8,256]{2,1,0:T(8,128)(2,1)S(1)} %copy-done.1), kind=kOutput, calls=%fused_computation.3 | convolution fusion | flops 3233807872 | bytes 14944256 | tf_op jit(solution)/shard_map/dot_general | solution.py:52
  152.4 23.6 %psum.23 = f32[512]{0:T(512)} all-reduce(f32[512]{0:T(512)S(1)} %multiply_reduce_fusion), channel_id=1, replica_groups=mesh['dom'=32,'mode'=16] {'mode'}, use_global_device_ids=true, to_apply=%region_5.7 | all-reduce | flops 512 | bytes 4096 | tf_op jit(solution)/shard_map/psum | solution.py:97
  (31 shorter events, 0.8 us)
Async XLA Ops:
  6.5 131.4 %all-gather.2.cloned.1.call-start = ((), (), s32[]{:S(2)}) async-start(), calls=%async_computation | async-start | bytes 4456448 | tf_op jit(solution)/shard_map/all_gather | solution.py:92
  9.2 15.4 %copy-start.2 = (f32[4096]{0:T(1024)S(1)}, f32[4096]{0:T(1024)}, u32[]{:S(2)}) copy-start(f32[4096]{0:T(1024)} %param.15) | copy-start | bytes 49156
  9.2 15.5 %copy-start.3 = (f32[4096]{0:T(1024)S(1)}, f32[4096]{0:T(1024)}, u32[]{:S(2)}) copy-start(f32[4096]{0:T(1024)} %param.14) | copy-start | bytes 49156
  9.2 15.5 %copy-start = (bf16[3,256,256]{2,1,0:T(8,128)(2,1)S(1)}, bf16[3,256,256]{2,1,0:T(8,128)(2,1)}, u32[]{:S(2)}) copy-start(bf16[3,256,256]{2,1,0:T(8,128)(2,1)} %param.11) | copy-start | bytes 1179652
  9.2 15.5 %copy-start.4 = (f32[256]{0:T(256)S(1)}, f32[256]{0:T(256)}, u32[]{:S(2)}) copy-start(f32[256]{0:T(256)} %param.12) | copy-start | bytes 3076
  9.3 12.0 %collective-permute-start = (bf16[3,64,256]{2,1,0:T(8,128)(2,1)S(1)}, bf16[3,64,256]{2,1,0:T(8,128)(2,1)S(1)}, u32[]{:S(2)}, u32[]{:S(2)}) collective-permute-start(bf16[3,64,256]{2,1,0:T(8,128)(2,1)S(1)} %select_bitcast_fusion.1), channel_id=1, source_target_pairs={{0,16},{16,32},{32,48},{48,64},{64,80},{80,96},{96,112},{112,128},... | collective-permute-start | bytes 294920 | tf_op jit(solution)/shard_map/ppermute | solution.py:12
  15.4 6.0 %collective-permute-start.1 = (bf16[3,64,256]{2,1,0:T(8,128)(2,1)S(1)}, bf16[3,64,256]{2,1,0:T(8,128)(2,1)S(1)}, u32[]{:S(2)}, u32[]{:S(2)}) collective-permute-start(bf16[3,64,256]{2,1,0:T(8,128)(2,1)S(1)} %select_bitcast_fusion), channel_id=1, source_target_pairs={{16,0},{32,16},{48,32},{64,48},{80,64},{96,80},{112,96},{128,112},... | collective-permute-start | bytes 294920 | tf_op jit(solution)/shard_map/ppermute | solution.py:15
  138.0 6.5 %copy-start.1 = (bf16[64,8,256]{2,1,0:T(8,128)(2,1)S(1)}, bf16[64,8,256]{2,1,0:T(8,128)(2,1)}, u32[]{:S(2)}) copy-start(bf16[64,8,256]{2,1,0:T(8,128)(2,1)} %fusion.1) | copy-start | bytes 786436
Sparse Core Ops, SparseCore 0:
  24.7 60.4 all-gather.1
where the time goes:
time: 183 us
  blocking collectives  125 us (68%)
  other arithmetic  21.8 us (12%)
  between operations  13.6 us (7%)
  matrix products  9.17 us (5%)
  local copies, waits for them, and re-layouts  7.77 us (4%)
  starting transfers between devices  5.38 us (3%)
    psum x1, blocking collectives, per_device(): lever_sum, general_sum = lax.psum((lever_arm, general), 'dom')  68.9 us
    all_gather x1, blocking collectives, per_device(): amplitudes = lax.all_gather(local_amps, 'mode', axis=1, tiled=True)  32.6 us
    psum x1, blocking collectives, per_device(): return lax.psum(partial_value, 'mode')  23.6 us
    dot_general x1, matrix products, block_terms(): projected = jnp.dot(own_forces, weights, preferred_element_type=jnp.float32)  7.9 us
    convert_element_type x1, other arithmetic, block_terms(): far_wide = far_forces.astype(jnp.float32)  6.54 us
    div x1, other arithmetic, correlation_block(): return top_part / bottom_part  5.04 us
    convert_element_type x1, other arithmetic, block_terms(): (amp_rows.T[:, :, None] * correlation[:, None, :] * amplitudes[None, :, :...  4.55 us
    ppermute x1, starting transfers between devices, extended_2(): lax.ppermute(lax.slice_in_dim(block, block.shape[dim] - width, None, axis...  4.08 us
  transfers between devices with their start and end apart: 3, of which 0 were waited for; matrix products, arithmetic and copies ran while one was open for 10% of the time, Pallas kernels for 0%

commit v1 on v0

v1 whole, which is shorter than its diff:
```python
import functools

import jax
import jax.numpy as jnp
from jax import lax
from jax.experimental import pallas as pl
from jax.experimental.pallas import tpu as pltpu
from jax.sharding import PartitionSpec as P

MESH = pl.DeviceIdType.MESH
F32 = jnp.float32
BF16 = jnp.bfloat16
CORES = 2


def dot(a, b):
    return jnp.dot(a, b, preferred_element_type=F32)


def offset_of(step):
    return ((step + 1) // 2) * (2 * (step % 2) - 1)


def kernel(
    dims,
    shapes_h, mass_h, spec_h, freq_h, damp_h, rec_h, conn_h, cnt_h, shd_h,
    out_ref,
    shapes, mass, spec, freq, damp, rec, conn, cnt, shd, codes, in_sem,
    half_u, rate_w, rows_u, rows_a, corr,
    halo_out, halo_in, halo_send, halo_recv,
    lev_own, lev_x, lev_z, lx_send, lx_recv, lz_send, lz_recv,
    onehot, recov, gathered, forces, far, f_send, f_recv,
    gain_own, gains, g_send, g_recv,
    scaled, total, res_own, results, r_send, r_recv,
):
    nz, nx, ny = dims
    n_dom, n_mode = nz * nx, ny * CORES
    block = shapes_h.shape[2]
    nodes = shapes_h.shape[1]
    elems = conn_h.shape[1]
    slots = conn_h.shape[0]
    share = shd_h.shape[1]
    comps = forces.shape[0]
    part = comps // n_mode
    wide = CORES * block

    dom = lax.axis_index("dom")
    mode = lax.axis_index("mode")
    zi, xi = dom // nx, dom % nx
    yi, core = mode // CORES, mode % CORES
    up = (dom + 1) % n_dom
    down = (dom + n_dom - 1) % n_dom

    def x_peer(k):
        return zi * nx + (xi + k) % nx

    def z_peer(k):
        return ((zi + k) % nz) * nx + xi

    barrier = pltpu.get_barrier_semaphore()

    def greet(d, m):
        pl.semaphore_signal(barrier, inc=1, device_id=(d, m), device_id_type=MESH)

    greet(up, mode)
    greet(down, mode)
    for k in range(1, nx):
        greet(x_peer(k), mode)
    for k in range(1, nz):
        greet(z_peer(k), mode)
    for k in range(1, n_mode):
        greet(dom, (mode + k) % n_mode)

    own = pl.multiple_of(mode * block, block)
    pairs = [
        (conn_h, conn),
        (cnt_h, cnt),
        (shd_h, shd),
        (shapes_h, shapes),
        (mass_h, mass),
        (spec_h.at[:, pl.ds(own, block)], spec),
        (freq_h, freq),
        (damp_h, damp),
        (rec_h, rec),
    ]
    loads = [pltpu.make_async_copy(a, b, in_sem.at[i]) for i, (a, b) in enumerate(pairs)]
    for load in loads:
        load.start()
    for load in loads:
        load.wait()

    codes[...] = jnp.zeros_like(codes)
    codes[pl.ds(0, slots), pl.ds(0, elems)] = conn[...].astype(F32)
    codes[pl.ds(slots, 1), pl.ds(0, elems)] = cnt[...].astype(F32)
    codes[pl.ds(slots + 1, 2), pl.ds(0, share)] = shd[...].astype(F32)
    columns = jnp.transpose(codes[...])
    node_lane = lax.broadcasted_iota(jnp.int32, (share, nodes), 1).astype(F32)
    pick = jnp.concatenate(
        [
            jnp.where(columns[0:share, slots + 1 + side : slots + 2 + side] == node_lane, 1.0, 0.0)
            for side in range(2)
        ],
        axis=0,
    ).astype(BF16)
    for d in range(3):
        halo_out[d] = dot(pick, shapes[d]).astype(BF16)

    m0 = mass[...]
    hi = m0.astype(BF16).astype(F32)
    mid = (m0 - hi).astype(BF16).astype(F32)
    low = m0 - hi - mid
    row8 = lax.broadcasted_iota(jnp.int32, (8, nodes), 0)
    mass3 = jnp.where(row8 == 0, hi, jnp.where(row8 == 1, mid, jnp.where(row8 == 2, low, 0.0)))
    mass3 = mass3.astype(BF16)
    terms = []
    square = jnp.zeros((8, block), F32)
    for d in range(3):
        terms.append(jnp.sum(dot(mass3, shapes[d]), axis=0, keepdims=True))
        s = shapes[d].astype(F32)
        s2 = s * s
        s2h = s2.astype(BF16)
        s2l = (s2 - s2h.astype(F32)).astype(BF16)
        square = square + dot(mass3, s2h) + dot(mass3, s2l)
    terms.append(jnp.sum(square, axis=0, keepdims=True))
    stack = jnp.concatenate(terms, axis=0)
    half = block // 2
    lev_own[...] = jnp.concatenate([stack[:, :half], stack[:, half:]], axis=0)

    pl.semaphore_wait(barrier, 2 + (nx - 1) + (nz - 1) + (n_mode - 1))

    halo_copies = [
        pltpu.make_async_remote_copy(
            src_ref=halo_out.at[:, pl.ds(share, share)],
            dst_ref=halo_in.at[:, pl.ds(0, share)],
            send_sem=halo_send.at[0],
            recv_sem=halo_recv.at[0],
            device_id=(up, mode),
            device_id_type=MESH,
        ),
        pltpu.make_async_remote_copy(
            src_ref=halo_out.at[:, pl.ds(0, share)],
            dst_ref=halo_in.at[:, pl.ds(share, share)],
            send_sem=halo_send.at[1],
            recv_sem=halo_recv.at[1],
            device_id=(down, mode),
            device_id_type=MESH,
        ),
    ]
    for copy in halo_copies:
        copy.start()
    x_copies = [
        pltpu.make_async_remote_copy(
            src_ref=lev_own,
            dst_ref=lev_x.at[k - 1],
            send_sem=lx_send.at[k - 1],
            recv_sem=lx_recv.at[k - 1],
            device_id=(x_peer(k), mode),
            device_id_type=MESH,
        )
        for k in range(1, nx)
    ]
    for copy in x_copies:
        copy.start()

    table_lane = lax.broadcasted_iota(jnp.int32, (elems, nodes + 2 * share), 1).astype(F32)
    for s in range(slots):
        code = columns[0:elems, s : s + 1]
        live = columns[0:elems, slots : slots + 1] > s
        is_low = jnp.logical_and(code >= nodes, code < nodes + share)
        is_high = code >= nodes + share
        ground_low = jnp.where(is_low, jnp.where(dom == 0, 1.0, 0.0), 0.0)
        ground_high = jnp.where(is_high, jnp.where(dom == n_dom - 1, 1.0, 0.0), 0.0)
        kept = jnp.where(live, 1.0, 0.0) * (1.0 - ground_low) * (1.0 - ground_high)
        code = jnp.where(kept > 0.5, code, -1.0)
        onehot[pl.ds(s * elems, elems)] = jnp.where(code == table_lane, 1.0, 0.0).astype(BF16)

    per = comps // elems
    rec_wide = rec[...].astype(F32)
    lane_elem = lax.broadcasted_iota(jnp.int32, rec_wide.shape, 1) % elems
    for e in range(0, elems, 2):
        recov[pl.ds(e * per, 2 * per)] = jnp.concatenate(
            [jnp.where(lane_elem == e + i, rec_wide, 0.0) for i in range(2)], axis=0
        ).astype(BF16)

    w = freq[...]
    half_u[...] = w * w * 0.25
    rate_w[...] = damp[...] * w
    groups = freq.shape[0]
    u_t = jnp.transpose(half_u[...])
    a_t = jnp.transpose(rate_w[...])
    for g in range(groups):
        rows_u[pl.ds(g * 128, 128)] = jnp.broadcast_to(u_t[:, g : g + 1], (128, 128))
        rows_a[pl.ds(g * 128, 128)] = jnp.broadcast_to(a_t[:, g : g + 1], (128, 128))

    def correlate(row_step, col_step):
        row_chip = (yi + offset_of(row_step) + ny) % ny
        col_chip = (yi + offset_of(col_step) + ny) % ny
        at = col_step * (col_step + 1) // 2 + row_step
        per_chip = wide // 128
        us = [half_u[pl.ds(col_chip * per_chip + g, 1)] for g in range(per_chip)]
        vs = [rate_w[pl.ds(col_chip * per_chip + g, 1)] for g in range(per_chip)]
        chunk = 64

        def rows(r, _):
            first = pl.multiple_of(row_chip * wide + r * chunk, chunk)
            u = rows_u[pl.ds(first, chunk)]
            a = rows_a[pl.ds(first, chunk)]
            for g in range(per_chip):
                gap = u - us[g]
                both = a + vs[g]
                bottom = gap * gap + both * (a * us[g] + vs[g] * u)
                value = both * pltpu.reciprocal(bottom, approx=True)
                corr[at, pl.ds(pl.multiple_of(r * chunk, chunk), chunk), pl.ds(g * 128, 128)] = (
                    value.astype(BF16)
                )
            return 0

        lax.fori_loop(0, wide // chunk, rows, 0)

    def correlate_columns(first, last):
        def column(t, _):
            def row(p, _):
                correlate(p, t)
                return 0

            lax.fori_loop(0, t + 1, row, 0)
            return 0

        lax.fori_loop(first, last, column, 0)

    parts = slots * elems
    for d in range(3):
        gathered[pl.ds(d * parts, parts)] = dot(onehot[:, pl.ds(0, nodes)], shapes[d]).astype(BF16)

    for copy in x_copies:
        copy.wait_recv()
    lev_sum = lev_own[...]
    for k in range(nx - 1):
        lev_sum = lev_sum + lev_x[k]
    lev_z[nz - 1] = lev_sum
    z_copies = [
        pltpu.make_async_remote_copy(
            src_ref=lev_z.at[nz - 1],
            dst_ref=lev_z.at[k - 1],
            send_sem=lz_send.at[k - 1],
            recv_sem=lz_recv.at[k - 1],
            device_id=(z_peer(k), mode),
            device_id_type=MESH,
        )
        for k in range(1, nz)
    ]
    for copy in z_copies:
        copy.start()

    for copy in halo_copies:
        copy.wait_recv()
    for d in range(3):
        far_part = dot(onehot[:, pl.ds(nodes, 2 * share)], halo_in[d]).astype(BF16)
        gathered[pl.ds(d * parts, parts)] = gathered[pl.ds(d * parts, parts)] + far_part
    forces[...] = dot(recov[...], gathered[...]).astype(BF16)

    def mode_of(step, c):
        return ((yi - offset_of(step) + ny) % ny) * CORES + c

    def far_copy(step, c):
        m = mode_of(step, c)
        return pltpu.make_async_remote_copy(
            src_ref=forces.at[pl.ds(pl.multiple_of(m * part, part), part)],
            dst_ref=far.at[step, core],
            send_sem=f_send.at[step, c],
            recv_sem=f_recv.at[step, core],
            device_id=(dom, m),
            device_id_type=MESH,
        )

    def gain_copy(step, c):
        m = mode_of(step, c)
        return pltpu.make_async_remote_copy(
            src_ref=gain_own.at[pl.ds(0, 6)],
            dst_ref=gains.at[step, core, pl.ds(0, 6)],
            send_sem=g_send.at[step, c],
            recv_sem=g_recv.at[step, core],
            device_id=(dom, m),
            device_id_type=MESH,
        )

    def arrival(buffer, sem, step, c):
        return pltpu.make_async_copy(buffer, buffer, sem.at[step, c])

    def start_all(make):
        make(0, 1 - core).start()

        def one(i, _):
            make(i // CORES, i % CORES).start()
            return 0

        lax.fori_loop(CORES, n_mode, one, 0)

    start_all(far_copy)
    far[0, core] = forces[pl.ds(pl.multiple_of(mode * part, part), part)]

    split = max(1, (ny * 5) // 8)
    correlate_columns(0, split)

    for copy in z_copies:
        copy.wait_recv()
    lev_all = lev_z[nz - 1]
    for k in range(nz - 1):
        lev_all = lev_all + lev_z[k]
    w2 = freq[pl.ds(mode * 2, 2)]
    scale2 = jnp.sqrt(0.5 * damp[pl.ds(mode * 2, 2)]) * (w2 * jnp.sqrt(w2))
    sp = spec[...]
    for h in range(2):
        rows = lev_all[4 * h : 4 * h + 3] / lev_all[4 * h + 3 : 4 * h + 4]
        rows = rows * sp[:, h * half : (h + 1) * half] * scale2[h : h + 1]
        gain_own[pl.ds(3 * h, 3)] = rows
    start_all(gain_copy)
    gains[0, core, pl.ds(0, 6)] = gain_own[pl.ds(0, 6)]

    correlate_columns(split, ny)

    total[...] = jnp.zeros_like(total)

    def combine(step):
        pieces = []
        for c in range(CORES):
            f = far[step, c].astype(F32)
            g = gains[step, c]
            for d in range(3):
                for h in range(2):
                    zz = f[:, h * half : (h + 1) * half] * g[3 * h + d : 3 * h + d + 1]
                    scaled[
                        step, pl.ds(d * part, part), pl.ds(c * block + h * half, half)
                    ] = zz.astype(BF16)

        def earlier(p, acc):
            at = step * (step + 1) // 2 + p
            return acc + dot(scaled[p], corr[at])

        acc = lax.fori_loop(0, step, earlier, jnp.zeros((3 * part, wide), F32))
        acc = acc * 2.0 + dot(scaled[step], corr[step * (step + 1) // 2 + step])
        acc = acc * scaled[step].astype(F32)
        add = acc[:, 0:128]
        for g in range(1, wide // 128):
            add = add + acc[:, g * 128 : (g + 1) * 128]
        total[...] += add

    arrival(far.at[0, 1 - core], f_recv, 0, 1 - core).wait()
    arrival(gains.at[0, 1 - core, pl.ds(0, 6)], g_recv, 0, 1 - core).wait()
    combine(0)

    def later(step, _):
        for c in range(CORES):
            arrival(far.at[step, c], f_recv, step, c).wait()
            arrival(gains.at[step, c, pl.ds(0, 6)], g_recv, step, c).wait()
        combine(step)
        return 0

    lax.fori_loop(1, ny, later, 0)

    t32 = total[pl.ds(0, part)]
    for d in range(1, 3):
        t32 = t32 + total[pl.ds(d * part, part)]
    copies = 128 // part
    turned = jnp.transpose(jnp.concatenate([t32] * copies, axis=0))
    line = jnp.sum(turned, axis=0, keepdims=True)
    lane = lax.broadcasted_iota(jnp.int32, (1, 128), 1)
    res_own[...] = jnp.where(lane // part == mode % copies, line, 0.0)
    results[pl.ds(mode, 1)] = res_own[...]

    def result_copy(k):
        return pltpu.make_async_remote_copy(
            src_ref=res_own,
            dst_ref=results.at[pl.ds(mode, 1)],
            send_sem=r_send.at[k],
            recv_sem=r_recv.at[mode],
            device_id=(dom, (mode + k) % n_mode),
            device_id_type=MESH,
        )

    def send_result(k, _):
        result_copy(k).start()
        return 0

    lax.fori_loop(1, n_mode, send_result, 0)

    def get_result(k, _):
        m = (mode + k) % n_mode
        row = results.at[pl.ds(m, 1)]
        pltpu.make_async_copy(row, row, r_recv.at[m]).wait()
        return 0

    lax.fori_loop(1, n_mode, get_result, 0)
    for i in range(n_mode // copies):
        out_ref[pl.ds(i, 1)] = jnp.sum(results[pl.ds(i * copies, copies)], axis=0, keepdims=True)

    for copy in halo_copies + x_copies + z_copies:
        copy.wait_send()

    def sent(i, _):
        far_copy(i // CORES, i % CORES).wait_send()
        gain_copy(i // CORES, i % CORES).wait_send()
        return 0

    far_copy(0, 1 - core).wait_send()
    gain_copy(0, 1 - core).wait_send()
    lax.fori_loop(CORES, n_mode, sent, 0)

    def result_sent(k, _):
        result_copy(k).wait_send()
        return 0

    lax.fori_loop(1, n_mode, result_sent, 0)


def per_device(
    dims, shapes, masses, spectral, frequencies, damping, recovery, connectivity, node_count, shared
):
    nz, nx, ny = dims
    n_mode = ny * CORES
    _, nodes, block = shapes.shape
    elems, slots = connectivity.shape
    per = recovery.shape[1]
    share = shared.shape[1]
    modes = frequencies.shape[0]
    comps = elems * per
    part = comps // n_mode
    wide = CORES * block
    parts = slots * elems
    groups = modes // 128
    dma = pltpu.SemaphoreType.DMA
    vmem = pltpu.VMEM
    scratch = [
        vmem((3, nodes, block), BF16),
        vmem((1, nodes), F32),
        vmem((3, block), F32),
        vmem((groups, 128), F32),
        vmem((groups, 128), F32),
        vmem((per, 3 * parts), BF16),
        vmem((slots, elems), jnp.int32),
        vmem((1, elems), jnp.int32),
        vmem((2, share), jnp.int32),
        vmem((8, 128), F32),
        dma((9,)),
        vmem((groups, 128), F32),
        vmem((groups, 128), F32),
        vmem((modes, 128), F32),
        vmem((modes, 128), F32),
        vmem((ny * (ny + 1) // 2, wide, wide), BF16),
        vmem((3, 2 * share, block), BF16),
        vmem((3, 2 * share, block), BF16),
        dma((2,)),
        dma((2,)),
        vmem((8, block // 2), F32),
        vmem((nx - 1, 8, block // 2), F32),
        vmem((nz, 8, block // 2), F32),
        dma((nx - 1,)),
        dma((nx - 1,)),
        dma((nz - 1,)),
        dma((nz - 1,)),
        vmem((parts, nodes + 2 * share), BF16),
        vmem((comps, 3 * parts), BF16),
        vmem((3 * parts, block), BF16),
        vmem((comps, block), BF16),
        vmem((ny, CORES, part, block), BF16),
        dma((ny, CORES)),
        dma((ny, CORES)),
        vmem((8, block // 2), F32),
        vmem((ny, CORES, 8, block // 2), F32),
        dma((ny, CORES)),
        dma((ny, CORES)),
        vmem((ny, 3 * part, wide), BF16),
        vmem((3 * part, 128), F32),
        vmem((1, 128), F32),
        vmem((n_mode, 128), F32),
        dma((n_mode,)),
        dma((n_mode,)),
    ]
    out = pl.pallas_call(
        functools.partial(kernel, dims),
        out_shape=jax.ShapeDtypeStruct((comps // 128, 128), F32),
        in_specs=[pl.BlockSpec(memory_space=pl.ANY)] * 9,
        out_specs=pl.BlockSpec(memory_space=pltpu.VMEM),
        scratch_shapes=scratch,
        compiler_params=pltpu.CompilerParams(
            collective_id=0, has_side_effects=True, vmem_limit_bytes=48 * 1024 * 1024
        ),
    )(
        shapes,
        masses.reshape(1, nodes),
        spectral,
        frequencies.reshape(groups, 128),
        damping.reshape(groups, 128),
        recovery.transpose(1, 3, 2, 0).reshape(per, 3 * parts),
        connectivity.transpose(1, 0),
        node_count.reshape(1, elems),
        shared,
    )
    return out.reshape(comps)


def solution(mesh, dims=(4, 8, 8)):
    in_specs = (
        P(None, "dom", "mode"),
        P("dom"),
        P(),
        P(),
        P(),
        P("dom", None, None, None),
        P("dom", None),
        P("dom"),
        P(None, "dom"),
    )
    return jax.shard_map(
        functools.partial(per_device, dims),
        mesh=mesh,
        in_specs=in_specs,
        out_specs=P("dom"),
        check_vma=False,
    )
```

time: 183 us -> 58 us (0.32)
  blocking collectives: 125 us -> 0 us
  Pallas kernels: 0 us -> 54.4 us
  other arithmetic: 21.8 us -> 0 us
  between operations: 13.6 us -> 0.09 us
  matrix products: 9.17 us -> 0 us
  starting transfers between devices: 5.38 us -> 0 us
  local copies, waits for them, and re-layouts: 7.77 us -> 3.32 us
    psum x2 -> x0, blocking collectives: 92.5 us -> none  [the longest x1 68.9 us: per_device(): lever_sum, general_sum = lax.psum((lever_arm, general), 'dom')]
    pallas_call x0 -> x1, Pallas kernels: none -> 54.4 us  [per_device(): pl.pallas_call(functools.partial(kernel, dims), out_shape=jax.ShapeDtypeS...]
    all_gather x1 -> x0, blocking collectives: 32.6 us -> none  [per_device(): amplitudes = lax.all_gather(local_amps, 'mode', axis=1, tiled=True)]
    convert_element_type x3 -> x0, other arithmetic: 11.8 us -> none  [the longest x1 6.54 us: block_terms(): far_wide = far_forces.astype(jnp.float32)]
    dot_general x2 -> x0, matrix products: 9.17 us -> none  [the longest x1 7.9 us: block_terms(): projected = jnp.dot(own_forces, weights, preferred_element_type=jnp.float32)]
    ppermute x2 -> x0, starting transfers between devices: 5.37 us -> none  [the longest x1 4.08 us: extended_2(): lax.ppermute(lax.slice_in_dim(block, block.shape[dim] - width, None, axis...]
    div x1 -> x0, other arithmetic: 5.04 us -> none  [correlation_block(): return top_part / bottom_part]
    gather x3 -> x0, local copies, waits for them, and re-layouts: 4.95 us -> none  [the longest x1 1.9 us: per_device(): jnp.take(shapes, shared[1], axis=1)]
  transfers between devices with their start and end apart: 3 -> 0, of which waited for: 0 -> 0; matrix products, arithmetic and copies ran while one was open for 10% -> 0% of each run, Pallas kernels for 0% -> 0%
where the time goes in v1:
time: 58 us; the launch traced here: 57.8 us
  Pallas kernels  54.4 us (94%)
  local copies, waits for them, and re-layouts  3.32 us (6%)
    pallas_call x1, Pallas kernels, per_device(): pl.pallas_call(functools.partial(kernel, dims), out_shape=jax.ShapeDtypeS...  54.4 us
    unnamed x17, local copies, waits for them, and re-layouts  2.43 us

profile of v1, /device:TPU:1, one launch (start us, length us, event | category | flops | bytes accessed | tf_op | source)
XLA Modules:
  0.0 57.8 jit_solution(4454125409498919390)
XLA Ops:
  0.0 0.0 copy-start.7
  0.0 0.0 copy-start.2
  0.0 0.0 copy-start.3
  0.0 0.0 copy-start.4
  0.0 0.0 copy-start.5
  0.0 0.0 copy-start.6
  0.0 0.9 %reshape.21.rec_h = bf16[8,768]{1,0:T(8,128)(2,1)S(1)} reshape(bf16[8,3,4,64]{3,2,1,0:T(4,128)(2,1)} %bitcast.13) | data formatting | bytes 24576 | tf_op jit(solution)/shard_map/reshape | solution.py:494
  0.9 0.0 copy-done.7
  0.9 0.0 copy-done.2
  0.9 0.0 copy-done.3
  0.9 0.0 copy-done.4
  1.0 0.0 copy-done.5
  1.0 0.0 copy-done.6
  1.0 0.0 copy-start
  1.0 1.0 %copy-done = bf16[3,256,256]{2,1,0:T(8,128)(2,1)S(1)} copy-done((bf16[3,256,256]{2,1,0:T(8,128)(2,1)S(1)}, bf16[3,256,256]{2,1,0:T(8,128)(2,1)}, u32[]{:S(2)}) %copy-start) | copy-done | bytes 393240
  2.0 0.0 copy-start.1
  2.0 0.8 %copy-done.1 = f32[3,4096]{1,0:T(4,128)S(1)} copy-done((f32[3,4096]{1,0:T(4,128)S(1)}, f32[3,4096]{1,0:T(4,128)}, u32[]{:S(2)}) %copy-start.1) | copy-done | bytes 49176
  2.8 54.4 %shard_map.91 = f32[4,128]{1,0:T(4,128)S(1)} custom-call(bf16[3,256,256]{2,1,0:T(8,128)(2,1)S(1)} %copy-done, f32[1,256]{1,0:T(1,128)S(1)} %bitcast.11, f32[3,4096]{1,0:T(4,128)S(1)} %copy-done.1, f32[32,128]{1,0:T(8,128)S(1)} %bitcast.7, f32[32,128]{1,0:T(8,128)S(1)} %bitcast.8, bf16[8,768]{1,0:T(8,128)(2,1)S(1)} %reshape.21.rec_h, s32[4,64]{1,0:T(4,128)S(1)} %bitcast.10, ...), custom_call_target="tpu_custom_call" | custom-call | tf_op jit(solution)/shard_map/pallas_call | solution.py:479
  57.2 0.6 %copy.11 = f32[512]{0:T(512)} copy(f32[512]{0:T(512)S(1)} %bitcast.9) | data formatting | bytes 4096
Async XLA Ops:
  0.0 0.9 %copy-start.7 = (s32[64]{0:T(128)S(1)}, s32[64]{0:T(128)}, u32[]{:S(2)}) copy-start(s32[64]{0:T(128)} %param.16) | copy-start | bytes 772
  0.0 0.9 %copy-start.2 = (f32[4096]{0:T(1024)S(1)}, f32[4096]{0:T(1024)}, u32[]{:S(2)}) copy-start(f32[4096]{0:T(1024)} %param.12) | copy-start | bytes 49156
  0.0 0.9 %copy-start.3 = (f32[4096]{0:T(1024)S(1)}, f32[4096]{0:T(1024)}, u32[]{:S(2)}) copy-start(f32[4096]{0:T(1024)} %param.13) | copy-start | bytes 49156
  0.0 0.9 %copy-start.4 = (s32[64,4]{0,1:T(4,128)S(1)}, s32[64,4]{0,1:T(4,128)}, u32[]{:S(2)}) copy-start(s32[64,4]{0,1:T(4,128)} %param.15) | copy-start | bytes 3076
  0.0 0.9 %copy-start.5 = (f32[256]{0:T(256)S(1)}, f32[256]{0:T(256)}, u32[]{:S(2)}) copy-start(f32[256]{0:T(256)} %param.10) | copy-start | bytes 3076
  0.0 0.9 %copy-start.6 = (s32[2,64]{1,0:T(2,128)S(1)}, s32[2,64]{1,0:T(2,128)}, u32[]{:S(2)}) copy-start(s32[2,64]{1,0:T(2,128)} %shd_h.1) | copy-start | bytes 1540
  1.0 1.0 %copy-start = (bf16[3,256,256]{2,1,0:T(8,128)(2,1)S(1)}, bf16[3,256,256]{2,1,0:T(8,128)(2,1)}, u32[]{:S(2)}) copy-start(bf16[3,256,256]{2,1,0:T(8,128)(2,1)} %shapes_h.1) | copy-start | bytes 1179652
  2.0 0.8 %copy-start.1 = (f32[3,4096]{1,0:T(4,128)S(1)}, f32[3,4096]{1,0:T(4,128)}, u32[]{:S(2)}) copy-start(f32[3,4096]{1,0:T(4,128)} %spec_h.1) | copy-start | bytes 147460

commit v2 on v1

--- a/solution.py
+++ b/solution.py
@@ -11,10 +11,20 @@
 F32 = jnp.float32
 BF16 = jnp.bfloat16
 CORES = 2
+FEATS = 32
+CHUNK = 512
 
 
 def dot(a, b):
     return jnp.dot(a, b, preferred_element_type=F32)
+
+
+def pieces_of(x, count):
+    parts = []
+    for _ in range(count):
+        parts.append(x.astype(BF16).astype(F32))
+        x = x - parts[-1]
+    return parts
 
 
 def offset_of(step):
@@ -25,8 +35,8 @@
     dims,
     shapes_h, mass_h, spec_h, freq_h, damp_h, rec_h, conn_h, cnt_h, shd_h,
     out_ref,
-    shapes, mass, spec, freq, damp, rec, conn, cnt, shd, codes, in_sem,
-    half_u, rate_w, rows_u, rows_a, corr,
+    shapes, mass, spec, freq, damp, rec, rec_rows, rec_line, conn, cnt, shd, codes, in_sem,
+    rate_w, row_feats, col_feats, row_mat, col_mat, rows_a, corr,
     halo_out, halo_in, halo_send, halo_recv,
     lev_own, lev_x, lev_z, lx_send, lx_recv, lz_send, lz_recv,
     onehot, recov, gathered, forces, far, f_send, f_recv,
@@ -175,47 +185,68 @@
         onehot[pl.ds(s * elems, elems)] = jnp.where(code == table_lane, 1.0, 0.0).astype(BF16)
 
     per = comps // elems
-    rec_wide = rec[...].astype(F32)
+    for k in range(per):
+        for d in range(3):
+            rec_rows[pl.ds(d * slots * per + k, slots, stride=per), pl.ds(0, elems)] = rec[k, d].astype(F32)
+    for i in range(3 * slots):
+        rec_line[:, pl.ds(i * elems, elems)] = rec_rows[pl.ds(i * per, per), pl.ds(0, elems)]
+    rec_wide = rec_line[...]
     lane_elem = lax.broadcasted_iota(jnp.int32, rec_wide.shape, 1) % elems
     for e in range(0, elems, 2):
         recov[pl.ds(e * per, 2 * per)] = jnp.concatenate(
             [jnp.where(lane_elem == e + i, rec_wide, 0.0) for i in range(2)], axis=0
         ).astype(BF16)
 
+    groups = freq.shape[0]
     w = freq[...]
-    half_u[...] = w * w * 0.25
-    rate_w[...] = damp[...] * w
-    groups = freq.shape[0]
-    u_t = jnp.transpose(half_u[...])
-    a_t = jnp.transpose(rate_w[...])
+    u = w * w * 0.25
+    rate = damp[...] * w
+    rate_w[...] = rate
+    one = jnp.ones_like(w)
+    square = pieces_of(u * u, 3)
+    u_h, u_m, u_l = pieces_of(u, 3)
+    rr_h, rr_m = pieces_of(rate * rate, 2)
+    ru_h, ru_m = pieces_of(rate * u, 2)
+    r_h, r_m = pieces_of(rate, 2)
+    left = [*square, one, one, one, u_h, u_h, u_m, u_m, u_h, u_l]
+    right = [one, one, one, *square] + [-2.0 * v for v in (u_h, u_m, u_h, u_m, u_l, u_h)]
+    for (p_h, p_m), (q_h, q_m) in (
+        ((rr_h, rr_m), (u_h, u_m)),
+        ((ru_h, ru_m), (r_h, r_m)),
+        ((r_h, r_m), (ru_h, ru_m)),
+        ((u_h, u_m), (rr_h, rr_m)),
+    ):
+        left += [p_h, p_h, p_m]
+        right += [q_h, q_m, q_h]
+    for feats, values in ((row_feats, left), (col_feats, right)):
+        for i in range(FEATS):
+            feats[pl.ds(i * groups, groups)] = values[i] if i < len(values) else jnp.zeros_like(w)
+    a_t = jnp.transpose(rate)
     for g in range(groups):
-        rows_u[pl.ds(g * 128, 128)] = jnp.broadcast_to(u_t[:, g : g + 1], (128, 128))
-        rows_a[pl.ds(g * 128, 128)] = jnp.broadcast_to(a_t[:, g : g + 1], (128, 128))
+        at = pl.ds(g * 128, 128)
+        row_mat[at] = jnp.transpose(row_feats[pl.ds(g, FEATS, stride=groups)]).astype(BF16)
+        col_mat[:, at] = col_feats[pl.ds(g, FEATS, stride=groups)].astype(BF16)
+        rows_a[at] = jnp.broadcast_to(a_t[:, g : g + 1], (128, 128))
 
     def correlate(row_step, col_step):
         row_chip = (yi + offset_of(row_step) + ny) % ny
         col_chip = (yi + offset_of(col_step) + ny) % ny
         at = col_step * (col_step + 1) // 2 + row_step
         per_chip = wide // 128
-        us = [half_u[pl.ds(col_chip * per_chip + g, 1)] for g in range(per_chip)]
         vs = [rate_w[pl.ds(col_chip * per_chip + g, 1)] for g in range(per_chip)]
-        chunk = 64
+        cols = col_mat[:, pl.ds(pl.multiple_of(col_chip * wide, wide), wide)]
 
         def rows(r, _):
-            first = pl.multiple_of(row_chip * wide + r * chunk, chunk)
-            u = rows_u[pl.ds(first, chunk)]
-            a = rows_a[pl.ds(first, chunk)]
+            first = pl.multiple_of(row_chip * wide + r * CHUNK, CHUNK)
+            bottom = dot(row_mat[pl.ds(first, CHUNK)], cols)
+            a = rows_a[pl.ds(first, CHUNK)]
+            to = pl.ds(pl.multiple_of(at * wide + r * CHUNK, CHUNK), CHUNK)
             for g in range(per_chip):
-                gap = u - us[g]
-                both = a + vs[g]
-                bottom = gap * gap + both * (a * us[g] + vs[g] * u)
-                value = both * pltpu.reciprocal(bottom, approx=True)
-                corr[at, pl.ds(pl.multiple_of(r * chunk, chunk), chunk), pl.ds(g * 128, 128)] = (
-                    value.astype(BF16)
-                )
+                value = (a + vs[g]) * pltpu.reciprocal(bottom[:, g * 128 : (g + 1) * 128], approx=True)
+                corr[to, pl.ds(g * 128, 128)] = value.astype(BF16)
             return 0
 
-        lax.fori_loop(0, wide // chunk, rows, 0)
+        lax.fori_loop(0, wide // CHUNK, rows, 0)
 
     def correlate_columns(first, last):
         def column(t, _):
@@ -330,16 +361,14 @@
                 for h in range(2):
                     zz = f[:, h * half : (h + 1) * half] * g[3 * h + d : 3 * h + d + 1]
                     scaled[
-                        step, pl.ds(d * part, part), pl.ds(c * block + h * half, half)
+                        pl.ds(d * part, part), pl.ds(step * wide + c * block + h * half, half)
                     ] = zz.astype(BF16)
-
-        def earlier(p, acc):
-            at = step * (step + 1) // 2 + p
-            return acc + dot(scaled[p], corr[at])
-
-        acc = lax.fori_loop(0, step, earlier, jnp.zeros((3 * part, wide), F32))
-        acc = acc * 2.0 + dot(scaled[step], corr[step * (step + 1) // 2 + step])
-        acc = acc * scaled[step].astype(F32)
+        at = step * (step + 1) // 2 * wide
+        here = pl.ds(step * wide, wide)
+        acc = dot(scaled[:, here], corr[pl.ds(at + step * wide, wide)])
+        if step:
+            acc = acc + 2.0 * dot(scaled[:, pl.ds(0, step * wide)], corr[pl.ds(at, step * wide)])
+        acc = acc * scaled[:, here].astype(F32)
         add = acc[:, 0:128]
         for g in range(1, wide // 128):
             add = add + acc[:, g * 128 : (g + 1) * 128]
@@ -349,14 +378,11 @@
     arrival(gains.at[0, 1 - core, pl.ds(0, 6)], g_recv, 0, 1 - core).wait()
     combine(0)
 
-    def later(step, _):
+    for step in range(1, ny):
         for c in range(CORES):
             arrival(far.at[step, c], f_recv, step, c).wait()
             arrival(gains.at[step, c, pl.ds(0, 6)], g_recv, step, c).wait()
         combine(step)
-        return 0
-
-    lax.fori_loop(1, ny, later, 0)
 
     t32 = total[pl.ds(0, part)]
     for d in range(1, 3):
@@ -436,17 +462,21 @@
         vmem((3, block), F32),
         vmem((groups, 128), F32),
         vmem((groups, 128), F32),
-        vmem((per, 3 * parts), BF16),
+        vmem((per, 3, slots, elems), BF16),
+        vmem((3 * slots * per, 128), F32),
+        vmem((per, 3 * parts), F32),
         vmem((slots, elems), jnp.int32),
         vmem((1, elems), jnp.int32),
         vmem((2, share), jnp.int32),
         vmem((8, 128), F32),
         dma((9,)),
         vmem((groups, 128), F32),
-        vmem((groups, 128), F32),
+        vmem((FEATS * groups, 128), F32),
+        vmem((FEATS * groups, 128), F32),
+        vmem((modes, FEATS), BF16),
+        vmem((FEATS, modes), BF16),
         vmem((modes, 128), F32),
-        vmem((modes, 128), F32),
-        vmem((ny * (ny + 1) // 2, wide, wide), BF16),
+        vmem((ny * (ny + 1) // 2 * wide, wide), BF16),
         vmem((3, 2 * share, block), BF16),
         vmem((3, 2 * share, block), BF16),
         dma((2,)),
@@ -469,7 +499,7 @@
         vmem((ny, CORES, 8, block // 2), F32),
         dma((ny, CORES)),
         dma((ny, CORES)),
-        vmem((ny, 3 * part, wide), BF16),
+        vmem((3 * part, modes), BF16),
         vmem((3 * part, 128), F32),
         vmem((1, 128), F32),
         vmem((n_mode, 128), F32),
@@ -479,7 +509,7 @@
     out = pl.pallas_call(
         functools.partial(kernel, dims),
         out_shape=jax.ShapeDtypeStruct((comps // 128, 128), F32),
-        in_specs=[pl.BlockSpec(memory_space=pl.ANY)] * 9,
+        in_specs=[pl.BlockSpec(memory_space=pltpu.HBM)] * 9,
         out_specs=pl.BlockSpec(memory_space=pltpu.VMEM),
         scratch_shapes=scratch,
         compiler_params=pltpu.CompilerParams(
@@ -491,7 +521,7 @@
         spectral,
         frequencies.reshape(groups, 128),
         damping.reshape(groups, 128),
-        recovery.transpose(1, 3, 2, 0).reshape(per, 3 * parts),
+        recovery.transpose(1, 3, 2, 0),
         connectivity.transpose(1, 0),
         node_count.reshape(1, elems),
         shared,

time: 58 us -> 48.5 us (0.84)
  Pallas kernels: 54.4 us -> 42.8 us
  local copies, waits for them, and re-layouts: 3.32 us -> 5.29 us
    pallas_call x1, Pallas kernels: 54.4 us -> 42.8 us  [per_device(): pl.pallas_call(functools.partial(kernel, dims), out_shape=jax.ShapeDtypeS...]
    unnamed x17 -> x19, local copies, waits for them, and re-layouts: 2.43 us -> 5.29 us
    reshape x1 -> x0, local copies, waits for them, and re-layouts: 0.89 us -> none  [per_device(): recovery.transpose(1, 3, 2, 0).reshape(per, 3 * parts)]
where the time goes in v2:
time: 48.5 us; the launch traced here: 48.1 us
  Pallas kernels  42.8 us (88%)
  local copies, waits for them, and re-layouts  5.29 us (11%)
    pallas_call x1, Pallas kernels, per_device(): pl.pallas_call(functools.partial(kernel, dims), out_shape=jax.ShapeDtypeS...  42.8 us
    unnamed x19, local copies, waits for them, and re-layouts  5.29 us

profile of v2, /device:TPU:1, one launch (start us, length us, event | category | flops | bytes accessed | tf_op | source)
XLA Modules:
  0.0 48.1 jit_solution(2035611548338479835)
XLA Ops:
  0.0 0.0 copy-start.7
  0.0 0.0 copy-start.5
  0.0 0.0 copy-start.6
  0.0 0.0 copy-start.8
  0.0 0.7 %copy-done.7 = s32[2,64]{1,0:T(2,128)S(1)} copy-done((s32[2,64]{1,0:T(2,128)S(1)}, s32[2,64]{1,0:T(2,128)}, u32[]{:S(2)}) %copy-start.7) | copy-done | bytes 536
  0.7 0.0 copy-done.5
  0.7 0.0 copy-done.6
  0.7 0.0 copy-done.8
  0.7 0.0 copy-start
  0.7 1.0 %copy-done = bf16[3,256,256]{2,1,0:T(8,128)(2,1)S(1)} copy-done((bf16[3,256,256]{2,1,0:T(8,128)(2,1)S(1)}, bf16[3,256,256]{2,1,0:T(8,128)(2,1)}, u32[]{:S(2)}) %copy-start) | copy-done | bytes 393240
  1.7 0.0 copy-start.1
  1.7 0.8 %copy-done.1 = f32[3,4096]{1,0:T(4,128)S(1)} copy-done((f32[3,4096]{1,0:T(4,128)S(1)}, f32[3,4096]{1,0:T(4,128)}, u32[]{:S(2)}) %copy-start.1) | copy-done | bytes 49176
  2.6 0.0 copy-start.2
  2.6 0.7 %copy-done.2 = bf16[64,8,4,3]{0,2,3,1:T(4,128)(2,1)S(1)} copy-done((bf16[64,8,4,3]{0,2,3,1:T(4,128)(2,1)S(1)}, bf16[64,8,4,3]{0,2,3,1:T(4,128)(2,1)}, u32[]{:S(2)}) %copy-start.2) | copy-done | bytes 12312
  3.3 0.0 copy-start.3
  3.3 0.7 %copy-done.3 = f32[4096]{0:T(1024)S(1)} copy-done((f32[4096]{0:T(1024)S(1)}, f32[4096]{0:T(1024)}, u32[]{:S(2)}) %copy-start.3) | copy-done | bytes 16408
  4.0 0.0 copy-start.4
  4.0 0.7 %copy-done.4 = f32[4096]{0:T(1024)S(1)} copy-done((f32[4096]{0:T(1024)S(1)}, f32[4096]{0:T(1024)}, u32[]{:S(2)}) %copy-start.4) | copy-done | bytes 16408
  4.7 42.8 %shard_map.91 = f32[4,128]{1,0:T(4,128)S(1)} custom-call(bf16[3,256,256]{2,1,0:T(8,128)(2,1)S(1)} %copy-done, f32[1,256]{1,0:T(1,128)S(1)} %bitcast.12, f32[3,4096]{1,0:T(4,128)S(1)} %copy-done.1, f32[32,128]{1,0:T(8,128)S(1)} %bitcast.8, f32[32,128]{1,0:T(8,128)S(1)} %bitcast.9, bf16[8,3,4,64]{3,2,1,0:T(4,128)(2,1)S(1)} %bitcast.7, s32[4,64]{1,0:T(4,128)S(1)} %bitcast.11, ...), custom_call_target="tpu_custom_call" | custom-call | tf_op jit(solution)/shard_map/pallas_call | solution.py:509
  47.6 0.6 %copy.11 = f32[512]{0:T(512)} copy(f32[512]{0:T(512)S(1)} %bitcast.10) | data formatting | bytes 4096
Async XLA Ops:
  0.0 0.7 %copy-start.7 = (s32[2,64]{1,0:T(2,128)S(1)}, s32[2,64]{1,0:T(2,128)}, u32[]{:S(2)}) copy-start(s32[2,64]{1,0:T(2,128)} %shd_h.1) | copy-start | bytes 1540
  0.0 0.7 %copy-start.5 = (s32[64,4]{0,1:T(4,128)S(1)}, s32[64,4]{0,1:T(4,128)}, u32[]{:S(2)}) copy-start(s32[64,4]{0,1:T(4,128)} %param.15) | copy-start | bytes 3076
  0.0 0.7 %copy-start.6 = (f32[256]{0:T(256)S(1)}, f32[256]{0:T(256)}, u32[]{:S(2)}) copy-start(f32[256]{0:T(256)} %param.10) | copy-start | bytes 3076
  0.0 0.7 %copy-start.8 = (s32[64]{0:T(128)S(1)}, s32[64]{0:T(128)}, u32[]{:S(2)}) copy-start(s32[64]{0:T(128)} %param.16) | copy-start | bytes 772
  0.7 1.0 %copy-start = (bf16[3,256,256]{2,1,0:T(8,128)(2,1)S(1)}, bf16[3,256,256]{2,1,0:T(8,128)(2,1)}, u32[]{:S(2)}) copy-start(bf16[3,256,256]{2,1,0:T(8,128)(2,1)} %shapes_h.1) | copy-start | bytes 1179652
  1.7 0.8 %copy-start.1 = (f32[3,4096]{1,0:T(4,128)S(1)}, f32[3,4096]{1,0:T(4,128)}, u32[]{:S(2)}) copy-start(f32[3,4096]{1,0:T(4,128)} %spec_h.1) | copy-start | bytes 147460
  2.6 0.7 %copy-start.2 = (bf16[64,8,4,3]{0,2,3,1:T(4,128)(2,1)S(1)}, bf16[64,8,4,3]{0,2,3,1:T(4,128)(2,1)}, u32[]{:S(2)}) copy-start(bf16[64,8,4,3]{0,2,3,1:T(4,128)(2,1)} %param.14) | copy-start | bytes 36868
  3.3 0.7 %copy-start.3 = (f32[4096]{0:T(1024)S(1)}, f32[4096]{0:T(1024)}, u32[]{:S(2)}) copy-start(f32[4096]{0:T(1024)} %param.12) | copy-start | bytes 49156
  4.0 0.7 %copy-start.4 = (f32[4096]{0:T(1024)S(1)}, f32[4096]{0:T(1024)}, u32[]{:S(2)}) copy-start(f32[4096]{0:T(1024)} %param.13) | copy-start | bytes 49156

commit v3 on v2

v3 whole, which is shorter than its diff:
```python
import functools

import jax
import jax.numpy as jnp
from jax import lax
from jax.experimental import pallas as pl
from jax.experimental.pallas import tpu as pltpu
from jax.sharding import PartitionSpec as P

MESH = pl.DeviceIdType.MESH
F32 = jnp.float32
BF16 = jnp.bfloat16
CORES = 2
FEATS = 32
RATE = 24
CHUNK = 256


def dot(a, b):
    return jnp.dot(a, b, preferred_element_type=F32)


def pieces_of(x, count):
    parts = []
    for _ in range(count):
        parts.append(x.astype(BF16).astype(F32))
        x = x - parts[-1]
    return parts


def offset_of(step):
    return ((step + 1) // 2) * (2 * (step % 2) - 1)


def remote(src, dst, send, recv, device):
    return pltpu.make_async_remote_copy(
        src_ref=src,
        dst_ref=dst,
        send_sem=send,
        recv_sem=recv,
        device_id=device,
        device_id_type=MESH,
    )


def kernel(
    dims,
    shapes_h, mass_h, spec_h, freq_h, damp_h, rec_h, conn_h, cnt_h, shd_h,
    out_ref,
    shapes, mass, spec, freq, damp, rec, rec_rows, rec_line, conn, cnt, shd, codes, in_sem,
    rate_w, row_feats, col_feats, row_mat, col_mat, rows_a, corr,
    halo_out, halo_in, halo_send, halo_recv,
    lev_own, lev_x, lev_z, lx_send, lx_recv, lz_send, lz_recv,
    onehot, recov, gathered, near, reach, forces,
    far, f_send, f_pass, f_recv,
    gain_own, gains, g_send, g_pass, g_recv,
    scaled, total, res_own, results, r_send, r_recv,
):
    nz, nx, ny = dims
    n_dom, n_mode = nz * nx, ny * CORES
    block = shapes_h.shape[2]
    half = block // 2
    nodes = shapes_h.shape[1]
    elems = conn_h.shape[1]
    slots = conn_h.shape[0]
    share = shd_h.shape[1]
    comps = forces.shape[0]
    part = comps // ny
    wide = CORES * block

    dom = lax.axis_index("dom")
    mode = lax.axis_index("mode")
    zi, xi = dom // nx, dom % nx
    yi, core = mode // CORES, mode % CORES
    other = 1 - core
    sibling = (dom, yi * CORES + other)
    up = (dom + 1) % n_dom
    down = (dom + n_dom - 1) % n_dom
    chips_from = [(yi + offset_of(s) + ny) % ny for s in range(ny)]
    chips_to = [(yi - offset_of(s) + ny) % ny for s in range(ny)]
    x_peers = [(zi * nx + (xi + k) % nx, mode) for k in range(1, nx)]
    z_peers = [(((zi + k) % nz) * nx + xi, mode) for k in range(1, nz)]
    mode_peers = [(dom, (mode + k) % n_mode) for k in range(1, n_mode)]

    own = pl.multiple_of(mode * block, block)
    pairs = [
        (conn_h, conn),
        (cnt_h, cnt),
        (shd_h, shd),
        (shapes_h, shapes),
        (mass_h, mass),
        (rec_h, rec),
        (freq_h, freq),
        (damp_h, damp),
        (spec_h.at[:, pl.ds(own, block)], spec),
    ]
    loads = [pltpu.make_async_copy(a, b, in_sem.at[i]) for i, (a, b) in enumerate(pairs)]
    for load in loads:
        load.start()

    barrier = pltpu.get_barrier_semaphore()
    greeted = [(up, mode), (down, mode)] + x_peers + z_peers + mode_peers
    for peer in greeted:
        pl.semaphore_signal(barrier, inc=1, device_id=peer, device_id_type=MESH)

    for load in loads[:4]:
        load.wait()

    codes[...] = jnp.zeros_like(codes)
    codes[pl.ds(0, slots), pl.ds(0, elems)] = conn[...].astype(F32)
    codes[pl.ds(slots, 1), pl.ds(0, elems)] = cnt[...].astype(F32)
    codes[pl.ds(slots + 1, 2), pl.ds(0, share)] = shd[...].astype(F32)
    columns = jnp.transpose(codes[...])
    node_lane = lax.broadcasted_iota(jnp.int32, (share, nodes), 1).astype(F32)
    pick = jnp.concatenate(
        [
            jnp.where(columns[0:share, slots + 1 + side : slots + 2 + side] == node_lane, 1.0, 0.0)
            for side in range(2)
        ],
        axis=0,
    ).astype(BF16)
    for d in range(3):
        halo_out[d] = dot(pick, shapes[d]).astype(BF16)

    pl.semaphore_wait(barrier, len(greeted))

    lower, upper = pl.ds(0, share), pl.ds(share, share)
    halo_copies = [
        remote(halo_out.at[:, upper], halo_in.at[:, lower], halo_send.at[0], halo_recv.at[0], (up, mode)),
        remote(halo_out.at[:, lower], halo_in.at[:, upper], halo_send.at[1], halo_recv.at[1], (down, mode)),
    ]
    for copy in halo_copies:
        copy.start()

    for load in loads[4:]:
        load.wait()
    parts3 = pieces_of(mass[...], 3)
    row8 = lax.broadcasted_iota(jnp.int32, (8, nodes), 0)
    mass3 = jnp.zeros((8, nodes), F32)
    for i in range(3):
        mass3 = jnp.where(row8 == i, parts3[i], mass3)
    mass3 = mass3.astype(BF16)
    terms = []
    square = jnp.zeros((8, block), F32)
    for d in range(3):
        terms.append(jnp.sum(dot(mass3, shapes[d]), axis=0, keepdims=True))
        s = shapes[d].astype(F32)
        s2h, s2l = pieces_of(s * s, 2)
        square = square + dot(mass3, s2h.astype(BF16)) + dot(mass3, s2l.astype(BF16))
    terms.append(jnp.sum(square, axis=0, keepdims=True))
    stack = jnp.concatenate(terms, axis=0)
    lev_own[...] = jnp.concatenate([stack[:, :half], stack[:, half:]], axis=0)

    x_copies = [
        remote(lev_own, lev_x.at[k], lx_send.at[k], lx_recv.at[k], peer)
        for k, peer in enumerate(x_peers)
    ]
    for copy in x_copies:
        copy.start()

    table_lane = lax.broadcasted_iota(jnp.int32, (elems, nodes + 2 * share), 1).astype(F32)
    for s in range(slots):
        code = columns[0:elems, s : s + 1]
        live = columns[0:elems, slots : slots + 1] > s
        is_low = jnp.logical_and(code >= nodes, code < nodes + share)
        is_high = code >= nodes + share
        ground_low = jnp.where(is_low, jnp.where(dom == 0, 1.0, 0.0), 0.0)
        ground_high = jnp.where(is_high, jnp.where(dom == n_dom - 1, 1.0, 0.0), 0.0)
        kept = jnp.where(live, 1.0, 0.0) * (1.0 - ground_low) * (1.0 - ground_high)
        code = jnp.where(kept > 0.5, code, -1.0)
        onehot[pl.ds(s * elems, elems)] = jnp.where(code == table_lane, 1.0, 0.0).astype(BF16)

    per = comps // elems
    for k in range(per):
        for d in range(3):
            rec_rows[pl.ds(d * slots * per + k, slots, stride=per), pl.ds(0, elems)] = rec[k, d].astype(F32)
    for i in range(3 * slots):
        rec_line[:, pl.ds(i * elems, elems)] = rec_rows[pl.ds(i * per, per), pl.ds(0, elems)]
    rec_wide = rec_line[...]
    lane_elem = lax.broadcasted_iota(jnp.int32, rec_wide.shape, 1) % elems
    for e in range(0, elems, 2):
        recov[pl.ds(e * per, 2 * per)] = jnp.concatenate(
            [jnp.where(lane_elem == e + i, rec_wide, 0.0) for i in range(2)], axis=0
        ).astype(BF16)

    parts = slots * elems
    for d in range(3):
        gathered[pl.ds(d * parts, parts)] = dot(onehot[:, pl.ds(0, nodes)], shapes[d]).astype(BF16)
        reach[:, pl.ds(d * 2 * share, 2 * share)] = dot(
            recov[:, pl.ds(d * parts, parts)], onehot[:, pl.ds(nodes, 2 * share)]
        ).astype(BF16)
    near[...] = dot(recov[...], gathered[...])

    groups = freq.shape[0]
    w = freq[...]
    u = w * w * 0.25
    rate = damp[...] * w
    rate_w[...] = rate
    one = jnp.ones_like(w)
    uu = pieces_of(u * u, 3)
    u_h, u_m, u_l = pieces_of(u, 3)
    rr = pieces_of(rate * rate, 2)
    ru = pieces_of(rate * u, 2)
    r1 = pieces_of(rate, 2)
    left = [*uu, one, one, one, u_h, u_h, u_m, u_m, u_h, u_l]
    right = [one, one, one, *uu] + [-2.0 * v for v in (u_h, u_m, u_h, u_m, u_l, u_h)]
    for (p_h, p_m), (q_h, q_m) in ((rr, (u_h, u_m)), (ru, r1), (r1, ru), ((u_h, u_m), rr)):
        left += [p_h, p_h, p_m]
        right += [q_h, q_m, q_h]
    zero = jnp.zeros_like(w)
    left += [rate] + [zero] * (FEATS - len(left) - 1)
    right += [zero] * (FEATS - len(right))
    for feats, values in ((row_feats, left), (col_feats, right)):
        for i in range(FEATS):
            feats[pl.ds(i * groups, groups)] = values[i]
    per_chip = wide // 128
    per_core = block // 128
    for step in range(ny):
        for j in range(per_chip):
            g = chips_from[step] * per_chip + j
            at = pl.ds(step * wide + j * 128, 128)
            turned = jnp.transpose(row_feats[pl.ds(g, FEATS, stride=groups)])
            row_mat[at] = turned.astype(BF16)
            rows_a[at] = jnp.broadcast_to(turned[:, RATE : RATE + 1], (128, 128))
        for j in range(per_core):
            g = chips_from[step] * per_chip + core * per_core + j
            col_mat[:, pl.ds(step * block + j * 128, 128)] = col_feats[
                pl.ds(g, FEATS, stride=groups)
            ].astype(BF16)

    def correlate(step):
        base = step * (step + 1) // 2 * wide
        vs = [
            rate_w[pl.ds(chips_from[step] * per_chip + core * per_core + j, 1)]
            for j in range(per_core)
        ]
        cols = col_mat[:, pl.ds(step * block, block)]
        for r in range(0, (step + 1) * wide, CHUNK):
            bottom = dot(row_mat[pl.ds(r, CHUNK)], cols)
            a = rows_a[pl.ds(r, CHUNK)]
            for j in range(per_core):
                value = (a + vs[j]) * pltpu.reciprocal(bottom[:, j * 128 : (j + 1) * 128], approx=True)
                corr[pl.ds(base + r, CHUNK), pl.ds(j * 128, 128)] = value.astype(BF16)

    for step in range(0, 3):
        correlate(step)

    for copy in halo_copies:
        copy.wait_recv()
    forces[...] = (near[...] + dot(reach[...], halo_in[...].reshape(6 * share, block))).astype(BF16)

    def rows_of(chip):
        return forces.at[pl.ds(pl.multiple_of(chip * part, part), part)]

    f_copies = [None] + [
        remote(
            rows_of(chips_to[s]),
            far.at[s, core],
            f_send.at[s],
            f_recv.at[s, core],
            (dom, chips_to[s] * CORES + core),
        )
        for s in range(1, ny)
    ]
    for copy in f_copies[1:]:
        copy.start()
    f_passes = [remote(rows_of(yi), far.at[0, core], f_pass.at[0], f_recv.at[0, core], sibling)] + [
        remote(far.at[s, core], far.at[s, core], f_pass.at[s], f_recv.at[s, core], sibling)
        for s in range(1, ny)
    ]
    f_passes[0].start()
    far[0, core] = forces[pl.ds(pl.multiple_of(yi * part, part), part)]

    for copy in x_copies:
        copy.wait_recv()
    lev_sum = lev_own[...]
    for k in range(nx - 1):
        lev_sum = lev_sum + lev_x[k]
    lev_z[nz - 1] = lev_sum
    z_copies = [
        remote(lev_z.at[nz - 1], lev_z.at[k], lz_send.at[k], lz_recv.at[k], peer)
        for k, peer in enumerate(z_peers)
    ]
    for copy in z_copies:
        copy.start()

    for step in range(3, min(5, ny)):
        correlate(step)

    for copy in z_copies:
        copy.wait_recv()
    lev_all = lev_z[nz - 1]
    for k in range(nz - 1):
        lev_all = lev_all + lev_z[k]
    w2 = freq[pl.ds(mode * per_core, per_core)]
    scale2 = jnp.sqrt(0.5 * damp[pl.ds(mode * per_core, per_core)]) * (w2 * jnp.sqrt(w2))
    sp = spec[...]
    for h in range(2):
        rows = lev_all[4 * h : 4 * h + 3] / lev_all[4 * h + 3 : 4 * h + 4]
        rows = rows * sp[:, h * half : (h + 1) * half] * scale2[h : h + 1]
        gain_own[pl.ds(3 * h, 3)] = rows
    six = pl.ds(0, 6)

    def gain_slot(s):
        return gains.at[s, core, six]

    g_copies = [None] + [
        remote(
            gain_own.at[six],
            gain_slot(s),
            g_send.at[s],
            g_recv.at[s, core],
            (dom, chips_to[s] * CORES + core),
        )
        for s in range(1, ny)
    ]
    for copy in g_copies[1:]:
        copy.start()
    g_passes = [remote(gain_own.at[six], gain_slot(0), g_pass.at[0], g_recv.at[0, core], sibling)] + [
        remote(gain_slot(s), gain_slot(s), g_pass.at[s], g_recv.at[s, core], sibling)
        for s in range(1, ny)
    ]
    g_passes[0].start()
    gains[0, core, six] = gain_own[six]

    def hand_on(s):
        f_copies[s].wait_recv()
        f_passes[s].start()

    def hand_on_gain(s):
        g_copies[s].wait_recv()
        g_passes[s].start()

    done = 1
    for step in range(5, ny):
        correlate(step)
        while done < ny and done <= 2 * (step - 4):
            hand_on(done)
            done += 1
    for s in range(1, ny):
        hand_on_gain(s)
    for s in range(done, ny):
        hand_on(s)

    total[...] = jnp.zeros_like(total)

    def arrival(buffer, sem):
        pltpu.make_async_copy(buffer, buffer, sem).wait()

    for step in range(ny):
        arrival(far.at[step, other], f_recv.at[step, other])
        arrival(gains.at[step, other, six], g_recv.at[step, other])
        for c in range(CORES):
            f = far[step, c].astype(F32)
            g = gains[step, c]
            for d in range(3):
                for h in range(2):
                    zz = f[:, h * half : (h + 1) * half] * g[3 * h + d : 3 * h + d + 1]
                    scaled[
                        pl.ds(d * part, part), pl.ds(step * wide + c * block + h * half, half)
                    ] = zz.astype(BF16)
        base = step * (step + 1) // 2 * wide
        acc = dot(scaled[:, pl.ds(step * wide, wide)], corr[pl.ds(base + step * wide, wide)])
        if step:
            acc = acc + 2.0 * dot(scaled[:, pl.ds(0, step * wide)], corr[pl.ds(base, step * wide)])
        mine = pl.ds(pl.multiple_of(step * wide + core * block, block), block)
        acc = acc * scaled[:, mine].astype(F32)
        add = acc[:, 0:128]
        for j in range(1, per_core):
            add = add + acc[:, j * 128 : (j + 1) * 128]
        total[...] += add

    summed = total[pl.ds(0, part)]
    for d in range(1, 3):
        summed = summed + total[pl.ds(d * part, part)]
    copies = 128 // part
    turned = jnp.transpose(jnp.concatenate([summed] * copies, axis=0))
    line = jnp.sum(turned, axis=0, keepdims=True)
    lane = lax.broadcasted_iota(jnp.int32, (1, 128), 1)
    res_own[...] = jnp.where(lane // part == yi % copies, line, 0.0)

    r_copies = [
        remote(res_own, results.at[pl.ds(mode, 1)], r_send.at[k], r_recv.at[mode], peer)
        for k, peer in enumerate(mode_peers)
    ]
    for copy in r_copies:
        copy.start()
    results[pl.ds(mode, 1)] = res_own[...]
    for _, m in mode_peers:
        arrival(results.at[pl.ds(m, 1)], r_recv.at[m])
    rows_each = n_mode * 128 // comps
    for i in range(comps // 128):
        out_ref[pl.ds(i, 1)] = jnp.sum(results[pl.ds(i * rows_each, rows_each)], axis=0, keepdims=True)

    for copy in halo_copies + x_copies + z_copies + f_copies[1:] + f_passes + g_copies[1:] + g_passes + r_copies:
        copy.wait_send()


def per_device(
    dims, shapes, masses, spectral, frequencies, damping, recovery, connectivity, node_count, shared
):
    nz, nx, ny = dims
    n_mode = ny * CORES
    _, nodes, block = shapes.shape
    elems, slots = connectivity.shape
    per = recovery.shape[1]
    share = shared.shape[1]
    modes = frequencies.shape[0]
    comps = elems * per
    part = comps // ny
    wide = CORES * block
    parts = slots * elems
    groups = modes // 128
    dma = pltpu.SemaphoreType.DMA
    vmem = pltpu.VMEM
    scratch = [
        vmem((3, nodes, block), BF16),
        vmem((1, nodes), F32),
        vmem((3, block), F32),
        vmem((groups, 128), F32),
        vmem((groups, 128), F32),
        vmem((per, 3, slots, elems), BF16),
        vmem((3 * slots * per, 128), F32),
        vmem((per, 3 * parts), F32),
        vmem((slots, elems), jnp.int32),
        vmem((1, elems), jnp.int32),
        vmem((2, share), jnp.int32),
        vmem((8, 128), F32),
        dma((9,)),
        vmem((groups, 128), F32),
        vmem((FEATS * groups, 128), F32),
        vmem((FEATS * groups, 128), F32),
        vmem((modes, FEATS), BF16),
        vmem((FEATS, modes // CORES), BF16),
        vmem((modes, 128), F32),
        vmem((ny * (ny + 1) // 2 * wide, block), BF16),
        vmem((3, 2 * share, block), BF16),
        vmem((3, 2 * share, block), BF16),
        dma((2,)),
        dma((2,)),
        vmem((8, block // 2), F32),
        vmem((nx - 1, 8, block // 2), F32),
        vmem((nz, 8, block // 2), F32),
        dma((nx - 1,)),
        dma((nx - 1,)),
        dma((nz - 1,)),
        dma((nz - 1,)),
        vmem((parts, nodes + 2 * share), BF16),
        vmem((comps, 3 * parts), BF16),
        vmem((3 * parts, block), BF16),
        vmem((comps, block), F32),
        vmem((comps, 6 * share), BF16),
        vmem((comps, block), BF16),
        vmem((ny, CORES, part, block), BF16),
        dma((ny,)),
        dma((ny,)),
        dma((ny, CORES)),
        vmem((8, block // 2), F32),
        vmem((ny, CORES, 8, block // 2), F32),
        dma((ny,)),
        dma((ny,)),
        dma((ny, CORES)),
        vmem((3 * part, modes), BF16),
        vmem((3 * part, 128), F32),
        vmem((1, 128), F32),
        vmem((n_mode, 128), F32),
        dma((n_mode - 1,)),
        dma((n_mode,)),
    ]
    out = pl.pallas_call(
        functools.partial(kernel, dims),
        out_shape=jax.ShapeDtypeStruct((comps // 128, 128), F32),
        in_specs=[pl.BlockSpec(memory_space=pltpu.HBM)] * 9,
        out_specs=pl.BlockSpec(memory_space=pltpu.VMEM),
        scratch_shapes=scratch,
        compiler_params=pltpu.CompilerParams(
            collective_id=0, has_side_effects=True, vmem_limit_bytes=56 * 1024 * 1024
        ),
    )(
        shapes,
        masses.reshape(1, nodes),
        spectral,
        frequencies.reshape(groups, 128),
        damping.reshape(groups, 128),
        recovery.transpose(1, 3, 2, 0),
        connectivity.transpose(1, 0),
        node_count.reshape(1, elems),
        shared,
    )
    return out.reshape(comps)


def solution(mesh, dims=(4, 8, 8)):
    in_specs = (
        P(None, "dom", "mode"),
        P("dom"),
        P(),
        P(),
        P(),
        P("dom", None, None, None),
        P("dom", None),
        P("dom"),
        P(None, "dom"),
    )
    return jax.shard_map(
        functools.partial(per_device, dims),
        mesh=mesh,
        in_specs=in_specs,
        out_specs=P("dom"),
        check_vma=False,
    )
```

time: 48.5 us -> 44.3 us (0.913)
  local copies, waits for them, and re-layouts: 5.29 us -> 1.26 us
    unnamed x19 -> x1, local copies, waits for them, and re-layouts: 5.29 us -> 1.26 us
where the time goes in v3:
time: 44.3 us; the launch traced here: 44.2 us
  Pallas kernels  42.9 us (97%)
  local copies, waits for them, and re-layouts  1.26 us (3%)
    pallas_call x1, Pallas kernels, per_device(): pl.pallas_call(functools.partial(kernel, dims), out_shape=jax.ShapeDtypeS...  42.9 us
    unnamed x1, local copies, waits for them, and re-layouts  1.26 us

profile of v3, /device:TPU:1, one launch (start us, length us, event | category | flops | bytes accessed | tf_op | source)
XLA Modules:
  0.0 44.2 jit_solution(2119330682849986413)
XLA Ops:
  0.0 42.9 %shard_map.91 = f32[4,128]{1,0:T(4,128)} custom-call(bf16[3,256,256]{2,1,0:T(8,128)(2,1)} %shapes_h.1, f32[1,256]{1,0:T(1,128)} %bitcast.12, f32[3,4096]{1,0:T(4,128)} %spec_h.1, f32[32,128]{1,0:T(8,128)} %bitcast.8, f32[32,128]{1,0:T(8,128)} %bitcast.9, bf16[8,3,4,64]{3,2,1,0:T(4,128)(2,1)} %bitcast.7, s32[4,64]{1,0:T(4,128)} %bitcast.11, ...), custom_call_target="tpu_custom_call" | custom-call | tf_op jit(solution)/shard_map/pallas_call | solution.py:470
  42.9 1.3 %copy.11 = f32[512]{0:T(512)} copy(f32[512]{0:T(512)} %bitcast.10) | data formatting | bytes 4096

commit v4 on v3

--- a/solution.py
+++ b/solution.py
@@ -28,8 +28,18 @@
     return parts
 
 
-def offset_of(step):
-    return ((step + 1) // 2) * (2 * (step % 2) - 1)
+def ring_order(count):
+    order = [0, count // 2]
+    for k in range((count - 1) // 2, 0, -1):
+        order += [k, -k]
+    return order[:count]
+
+
+def around(at, by, count):
+    if by == 0:
+        return at
+    moved = at + by
+    return jnp.where(moved >= count, moved - count, moved) if by > 0 else jnp.where(moved < 0, moved + count, moved)
 
 
 def remote(src, dst, send, recv, device):
@@ -53,8 +63,8 @@
     lev_own, lev_x, lev_z, lx_send, lx_recv, lz_send, lz_recv,
     onehot, recov, gathered, near, reach, forces,
     far, f_send, f_pass, f_recv,
-    gain_own, gains, g_send, g_pass, g_recv,
-    scaled, total, res_own, results, r_send, r_recv,
+    gain_own, gains, g_send, g_recv,
+    scaled, total, res_own, r_send, r_recv,
 ):
     nz, nx, ny = dims
     n_dom, n_mode = nz * nx, ny * CORES
@@ -70,17 +80,17 @@
 
     dom = lax.axis_index("dom")
     mode = lax.axis_index("mode")
-    zi, xi = dom // nx, dom % nx
-    yi, core = mode // CORES, mode % CORES
+    zi, yi = lax.div(dom, nx), lax.div(mode, CORES)
+    xi, core = dom - zi * nx, mode - yi * CORES
     other = 1 - core
     sibling = (dom, yi * CORES + other)
-    up = (dom + 1) % n_dom
-    down = (dom + n_dom - 1) % n_dom
-    chips_from = [(yi + offset_of(s) + ny) % ny for s in range(ny)]
-    chips_to = [(yi - offset_of(s) + ny) % ny for s in range(ny)]
-    x_peers = [(zi * nx + (xi + k) % nx, mode) for k in range(1, nx)]
-    z_peers = [(((zi + k) % nz) * nx + xi, mode) for k in range(1, nz)]
-    mode_peers = [(dom, (mode + k) % n_mode) for k in range(1, n_mode)]
+    up = around(dom, 1, n_dom)
+    down = around(dom, -1, n_dom)
+    chips_from = [around(yi, k, ny) for k in ring_order(ny)]
+    chips_to = [around(yi, -k, ny) for k in ring_order(ny)]
+    x_peers = [(zi * nx + around(xi, k, nx), mode) for k in ring_order(nx)[1:]]
+    z_peers = [(around(zi, k, nz) * nx + xi, mode) for k in ring_order(nz)[1:]]
+    mode_peers = [(dom, chip * CORES + c) for chip in chips_to[1:] for c in range(CORES)] + [sibling]
 
     own = pl.multiple_of(mode * block, block)
     pairs = [
@@ -95,44 +105,17 @@
         (spec_h.at[:, pl.ds(own, block)], spec),
     ]
     loads = [pltpu.make_async_copy(a, b, in_sem.at[i]) for i, (a, b) in enumerate(pairs)]
-    for load in loads:
+    for load in loads[:5]:
         load.start()
 
     barrier = pltpu.get_barrier_semaphore()
-    greeted = [(up, mode), (down, mode)] + x_peers + z_peers + mode_peers
+    greeted = z_peers + mode_peers[:2] + x_peers + mode_peers[2:] + [(up, mode), (down, mode)]
     for peer in greeted:
         pl.semaphore_signal(barrier, inc=1, device_id=peer, device_id_type=MESH)
-
-    for load in loads[:4]:
-        load.wait()
-
-    codes[...] = jnp.zeros_like(codes)
-    codes[pl.ds(0, slots), pl.ds(0, elems)] = conn[...].astype(F32)
-    codes[pl.ds(slots, 1), pl.ds(0, elems)] = cnt[...].astype(F32)
-    codes[pl.ds(slots + 1, 2), pl.ds(0, share)] = shd[...].astype(F32)
-    columns = jnp.transpose(codes[...])
-    node_lane = lax.broadcasted_iota(jnp.int32, (share, nodes), 1).astype(F32)
-    pick = jnp.concatenate(
-        [
-            jnp.where(columns[0:share, slots + 1 + side : slots + 2 + side] == node_lane, 1.0, 0.0)
-            for side in range(2)
-        ],
-        axis=0,
-    ).astype(BF16)
-    for d in range(3):
-        halo_out[d] = dot(pick, shapes[d]).astype(BF16)
-
-    pl.semaphore_wait(barrier, len(greeted))
-
-    lower, upper = pl.ds(0, share), pl.ds(share, share)
-    halo_copies = [
-        remote(halo_out.at[:, upper], halo_in.at[:, lower], halo_send.at[0], halo_recv.at[0], (up, mode)),
-        remote(halo_out.at[:, lower], halo_in.at[:, upper], halo_send.at[1], halo_recv.at[1], (down, mode)),
-    ]
-    for copy in halo_copies:
-        copy.start()
-
-    for load in loads[4:]:
+    for load in loads[5:]:
+        load.start()
+
+    for load in loads[:5]:
         load.wait()
     parts3 = pieces_of(mass[...], 3)
     row8 = lax.broadcasted_iota(jnp.int32, (8, nodes), 0)
@@ -151,6 +134,24 @@
     stack = jnp.concatenate(terms, axis=0)
     lev_own[...] = jnp.concatenate([stack[:, :half], stack[:, half:]], axis=0)
 
+
+    codes[...] = jnp.zeros_like(codes)
+    codes[pl.ds(0, slots), pl.ds(0, elems)] = conn[...].astype(F32)
+    codes[pl.ds(slots, 1), pl.ds(0, elems)] = cnt[...].astype(F32)
+    codes[pl.ds(slots + 1, 2), pl.ds(0, share)] = shd[...].astype(F32)
+    columns = jnp.transpose(codes[...])
+    node_lane = lax.broadcasted_iota(jnp.int32, (share, nodes), 1).astype(F32)
+    pick = jnp.concatenate(
+        [
+            jnp.where(columns[0:share, slots + 1 + side : slots + 2 + side] == node_lane, 1.0, 0.0)
+            for side in range(2)
+        ],
+        axis=0,
+    ).astype(BF16)
+    for d in range(3):
+        halo_out[d] = dot(pick, shapes[d]).astype(BF16)
+
+    pl.semaphore_wait(barrier, len(greeted))
     x_copies = [
         remote(lev_own, lev_x.at[k], lx_send.at[k], lx_recv.at[k], peer)
         for k, peer in enumerate(x_peers)
@@ -158,6 +159,17 @@
     for copy in x_copies:
         copy.start()
 
+
+    lower, upper = pl.ds(0, share), pl.ds(share, share)
+    halo_copies = [
+        remote(halo_out.at[:, upper], halo_in.at[:, lower], halo_send.at[0], halo_recv.at[0], (up, mode)),
+        remote(halo_out.at[:, lower], halo_in.at[:, upper], halo_send.at[1], halo_recv.at[1], (down, mode)),
+    ]
+    for copy in halo_copies:
+        copy.start()
+
+    for load in loads[5:]:
+        load.wait()
     table_lane = lax.broadcasted_iota(jnp.int32, (elems, nodes + 2 * share), 1).astype(F32)
     for s in range(slots):
         code = columns[0:elems, s : s + 1]
@@ -284,7 +296,7 @@
     for copy in z_copies:
         copy.start()
 
-    for step in range(3, min(5, ny)):
+    for step in range(3, min(8, ny)):
         correlate(step)
 
     for copy in z_copies:
@@ -301,55 +313,40 @@
         gain_own[pl.ds(3 * h, 3)] = rows
     six = pl.ds(0, 6)
 
-    def gain_slot(s):
-        return gains.at[s, core, six]
-
-    g_copies = [None] + [
+    g_copies = [
         remote(
             gain_own.at[six],
-            gain_slot(s),
-            g_send.at[s],
-            g_recv.at[s, core],
-            (dom, chips_to[s] * CORES + core),
+            gains.at[t, core, six],
+            g_send.at[t, c],
+            g_recv.at[t, core],
+            (dom, chips_to[t] * CORES + c),
         )
-        for s in range(1, ny)
-    ]
-    for copy in g_copies[1:]:
+        for t in range(1, ny)
+        for c in range(CORES)
+    ] + [remote(gain_own.at[six], gains.at[0, core, six], g_send.at[0, 0], g_recv.at[0, core], sibling)]
+    for copy in g_copies:
         copy.start()
-    g_passes = [remote(gain_own.at[six], gain_slot(0), g_pass.at[0], g_recv.at[0, core], sibling)] + [
-        remote(gain_slot(s), gain_slot(s), g_pass.at[s], g_recv.at[s, core], sibling)
-        for s in range(1, ny)
-    ]
-    g_passes[0].start()
     gains[0, core, six] = gain_own[six]
 
     def hand_on(s):
         f_copies[s].wait_recv()
         f_passes[s].start()
 
-    def hand_on_gain(s):
-        g_copies[s].wait_recv()
-        g_passes[s].start()
-
-    done = 1
-    for step in range(5, ny):
+    for step in range(8, ny):
         correlate(step)
-        while done < ny and done <= 2 * (step - 4):
-            hand_on(done)
-            done += 1
-    for s in range(1, ny):
-        hand_on_gain(s)
-    for s in range(done, ny):
-        hand_on(s)
-
     total[...] = jnp.zeros_like(total)
 
     def arrival(buffer, sem):
         pltpu.make_async_copy(buffer, buffer, sem).wait()
 
     for step in range(ny):
+        for s in range(step + 2, min(step + 3, ny)) if step else range(1, min(3, ny)):
+            hand_on(s)
         arrival(far.at[step, other], f_recv.at[step, other])
-        arrival(gains.at[step, other, six], g_recv.at[step, other])
+        for c in range(CORES) if step else ():
+            arrival(gains.at[step, c, six], g_recv.at[step, c])
+        if step == 0:
+            arrival(gains.at[0, other, six], g_recv.at[0, other])
         for c in range(CORES):
             f = far[step, c].astype(F32)
             g = gains[step, c]
@@ -377,22 +374,22 @@
     turned = jnp.transpose(jnp.concatenate([summed] * copies, axis=0))
     line = jnp.sum(turned, axis=0, keepdims=True)
     lane = lax.broadcasted_iota(jnp.int32, (1, 128), 1)
-    res_own[...] = jnp.where(lane // part == yi % copies, line, 0.0)
+    res_own[...] = jnp.where(lane // part == yi - lax.div(yi, copies) * copies, line, 0.0)
 
     r_copies = [
-        remote(res_own, results.at[pl.ds(mode, 1)], r_send.at[k], r_recv.at[mode], peer)
+        remote(res_own, out_ref.at[pl.ds(mode, 1)], r_send.at[k], r_recv.at[mode], peer)
         for k, peer in enumerate(mode_peers)
     ]
     for copy in r_copies:
         copy.start()
-    results[pl.ds(mode, 1)] = res_own[...]
+    keep = pltpu.make_async_copy(res_own, out_ref.at[pl.ds(mode, 1)], r_recv.at[mode])
+    keep.start()
+    for copy in halo_copies + x_copies + z_copies + f_copies[1:] + f_passes + g_copies:
+        copy.wait_send()
     for _, m in mode_peers:
-        arrival(results.at[pl.ds(m, 1)], r_recv.at[m])
-    rows_each = n_mode * 128 // comps
-    for i in range(comps // 128):
-        out_ref[pl.ds(i, 1)] = jnp.sum(results[pl.ds(i * rows_each, rows_each)], axis=0, keepdims=True)
-
-    for copy in halo_copies + x_copies + z_copies + f_copies[1:] + f_passes + g_copies[1:] + g_passes + r_copies:
+        arrival(out_ref.at[pl.ds(m, 1)], r_recv.at[m])
+    keep.wait()
+    for copy in r_copies:
         copy.wait_send()
 
 
@@ -457,21 +454,19 @@
         dma((ny, CORES)),
         vmem((8, block // 2), F32),
         vmem((ny, CORES, 8, block // 2), F32),
-        dma((ny,)),
-        dma((ny,)),
+        dma((ny, CORES)),
         dma((ny, CORES)),
         vmem((3 * part, modes), BF16),
         vmem((3 * part, 128), F32),
         vmem((1, 128), F32),
-        vmem((n_mode, 128), F32),
         dma((n_mode - 1,)),
         dma((n_mode,)),
     ]
     out = pl.pallas_call(
         functools.partial(kernel, dims),
-        out_shape=jax.ShapeDtypeStruct((comps // 128, 128), F32),
+        out_shape=jax.ShapeDtypeStruct((n_mode, 128), F32),
         in_specs=[pl.BlockSpec(memory_space=pltpu.HBM)] * 9,
-        out_specs=pl.BlockSpec(memory_space=pltpu.VMEM),
+        out_specs=pl.BlockSpec(memory_space=pltpu.HBM),
         scratch_shapes=scratch,
         compiler_params=pltpu.CompilerParams(
             collective_id=0, has_side_effects=True, vmem_limit_bytes=56 * 1024 * 1024
@@ -487,7 +482,7 @@
         node_count.reshape(1, elems),
         shared,
     )
-    return out.reshape(comps)
+    return jnp.sum(out.reshape(comps // 128, n_mode * 128 // comps, 128), axis=1).reshape(comps)
 
 
 def solution(mesh, dims=(4, 8, 8)):

time: 44.3 us -> 43.2 us (0.975)
  other arithmetic: 0 us -> 1.29 us
  local copies, waits for them, and re-layouts: 1.26 us -> 0 us
  Pallas kernels: 42.9 us -> 41.7 us
    reduce_sum x0 -> x1, other arithmetic: none -> 1.29 us  [per_device(): jnp.sum(out.reshape(comps // 128, n_mode * 128 // comps, 128), axis=1)]
    unnamed x1 -> x0, local copies, waits for them, and re-layouts: 1.26 us -> none
    pallas_call x1, Pallas kernels: 42.9 us -> 41.7 us  [per_device(): pl.pallas_call(functools.partial(kernel, dims), out_shape=jax.ShapeDtypeS...]
where the time goes in v4:
time: 43.2 us; the launch traced here: 43 us
  Pallas kernels  41.7 us (97%)
  other arithmetic  1.29 us (3%)
    pallas_call x1, Pallas kernels, per_device(): pl.pallas_call(functools.partial(kernel, dims), out_shape=jax.ShapeDtypeS...  41.7 us
    reduce_sum x1, other arithmetic, per_device(): jnp.sum(out.reshape(comps // 128, n_mode * 128 // comps, 128), axis=1)  1.29 us

profile of v4, /device:TPU:1, one launch (start us, length us, event | category | flops | bytes accessed | tf_op | source)
XLA Modules:
  0.0 43.0 jit_solution(16917128268984557994)
XLA Ops:
  0.0 41.7 %shard_map.91 = f32[16,128]{1,0:T(8,128)} custom-call(bf16[3,256,256]{2,1,0:T(8,128)(2,1)} %shapes_h.1, f32[1,256]{1,0:T(1,128)} %bitcast.13, f32[3,4096]{1,0:T(4,128)} %spec_h.1, f32[32,128]{1,0:T(8,128)} %bitcast.10, f32[32,128]{1,0:T(8,128)} %bitcast.11, bf16[8,3,4,64]{3,2,1,0:T(4,128)(2,1)} %bitcast.9, s32[4,64]{1,0:T(4,128)} %bitcast.12, ...), custom_call_target="tpu_custom_call" | custom-call | tf_op jit(solution)/shard_map/pallas_call | solution.py:465
  41.7 1.3 %reduce_sum.9 = f32[4,128]{1,0:T(4,128)} reduce(f32[4,4,128]{2,1,0:T(4,128)} %bitcast.8, f32[]{:T(128)} %constant.0.clone.1), dimensions={1}, to_apply=%region_0.0 | reduce | flops 1536 | bytes 10244 | tf_op jit(solution)/shard_map/reduce_sum | solution.py:485

commit v5 on v4

--- a/solution.py
+++ b/solution.py
@@ -152,14 +152,6 @@
         halo_out[d] = dot(pick, shapes[d]).astype(BF16)
 
     pl.semaphore_wait(barrier, len(greeted))
-    x_copies = [
-        remote(lev_own, lev_x.at[k], lx_send.at[k], lx_recv.at[k], peer)
-        for k, peer in enumerate(x_peers)
-    ]
-    for copy in x_copies:
-        copy.start()
-
-
     lower, upper = pl.ds(0, share), pl.ds(share, share)
     halo_copies = [
         remote(halo_out.at[:, upper], halo_in.at[:, lower], halo_send.at[0], halo_recv.at[0], (up, mode)),
@@ -167,6 +159,13 @@
     ]
     for copy in halo_copies:
         copy.start()
+    x_copies = [
+        remote(lev_own, lev_x.at[k], lx_send.at[k], lx_recv.at[k], peer)
+        for k, peer in enumerate(x_peers)
+    ]
+    for copy in x_copies:
+        copy.start()
+
 
     for load in loads[5:]:
         load.wait()

time: 43.2 us -> 43.2 us (level)
  no operation moved by 1% of the time
where the time goes in v5:
time: 43.2 us; the launch traced here: 43 us
  Pallas kernels  41.7 us (97%)
  other arithmetic  1.29 us (3%)
    pallas_call x1, Pallas kernels, per_device(): pl.pallas_call(functools.partial(kernel, dims), out_shape=jax.ShapeDtypeS...  41.7 us
    reduce_sum x1, other arithmetic, per_device(): jnp.sum(out.reshape(comps // 128, n_mode * 128 // comps, 128), axis=1)  1.29 us

profile of v5, /device:TPU:1, one launch (start us, length us, event | category | flops | bytes accessed | tf_op | source)
XLA Modules:
  0.0 43.0 jit_solution(4718057547962726819)
XLA Ops:
  0.0 41.7 %shard_map.91 = f32[16,128]{1,0:T(8,128)} custom-call(bf16[3,256,256]{2,1,0:T(8,128)(2,1)} %shapes_h.1, f32[1,256]{1,0:T(1,128)} %bitcast.13, f32[3,4096]{1,0:T(4,128)} %spec_h.1, f32[32,128]{1,0:T(8,128)} %bitcast.10, f32[32,128]{1,0:T(8,128)} %bitcast.11, bf16[8,3,4,64]{3,2,1,0:T(4,128)(2,1)} %bitcast.9, s32[4,64]{1,0:T(4,128)} %bitcast.12, ...), custom_call_target="tpu_custom_call" | custom-call | tf_op jit(solution)/shard_map/pallas_call | solution.py:464
  41.7 1.3 %reduce_sum.9 = f32[4,128]{1,0:T(4,128)} reduce(f32[4,4,128]{2,1,0:T(4,128)} %bitcast.8, f32[]{:T(128)} %constant.0.clone.1), dimensions={1}, to_apply=%region_0.0 | reduce | flops 1536 | bytes 10244 | tf_op jit(solution)/shard_map/reduce_sum | solution.py:484

commit v6 on v4

--- a/solution.py
+++ b/solution.py
@@ -334,14 +334,14 @@
 
     for step in range(8, ny):
         correlate(step)
+    for s in range(1, ny):
+        hand_on(s)
     total[...] = jnp.zeros_like(total)
 
     def arrival(buffer, sem):
         pltpu.make_async_copy(buffer, buffer, sem).wait()
 
     for step in range(ny):
-        for s in range(step + 2, min(step + 3, ny)) if step else range(1, min(3, ny)):
-            hand_on(s)
         arrival(far.at[step, other], f_recv.at[step, other])
         for c in range(CORES) if step else ():
             arrival(gains.at[step, c, six], g_recv.at[step, c])

time: 43.2 us -> 43.2 us (level)
  no operation moved by 1% of the time
where the time goes in v6:
time: 43.2 us; the launch traced here: 43 us
  Pallas kernels  41.7 us (97%)
  other arithmetic  1.29 us (3%)
    pallas_call x1, Pallas kernels, per_device(): pl.pallas_call(functools.partial(kernel, dims), out_shape=jax.ShapeDtypeS...  41.7 us
    reduce_sum x1, other arithmetic, per_device(): jnp.sum(out.reshape(comps // 128, n_mode * 128 // comps, 128), axis=1)  1.29 us

profile of v6, /device:TPU:1, one launch (start us, length us, event | category | flops | bytes accessed | tf_op | source)
XLA Modules:
  0.0 43.0 jit_solution(3959542094373844316)
XLA Ops:
  0.0 41.7 %shard_map.91 = f32[16,128]{1,0:T(8,128)} custom-call(bf16[3,256,256]{2,1,0:T(8,128)(2,1)} %shapes_h.1, f32[1,256]{1,0:T(1,128)} %bitcast.13, f32[3,4096]{1,0:T(4,128)} %spec_h.1, f32[32,128]{1,0:T(8,128)} %bitcast.10, f32[32,128]{1,0:T(8,128)} %bitcast.11, bf16[8,3,4,64]{3,2,1,0:T(4,128)(2,1)} %bitcast.9, s32[4,64]{1,0:T(4,128)} %bitcast.12, ...), custom_call_target="tpu_custom_call" | custom-call | tf_op jit(solution)/shard_map/pallas_call | solution.py:465
  41.7 1.3 %reduce_sum.9 = f32[4,128]{1,0:T(4,128)} reduce(f32[4,4,128]{2,1,0:T(4,128)} %bitcast.8, f32[]{:T(128)} %constant.0.clone.1), dimensions={1}, to_apply=%region_0.0 | reduce | flops 1536 | bytes 10244 | tf_op jit(solution)/shard_map/reduce_sum | solution.py:485
